TPU v7x, 256 devices: a whole 4x4x8 slice. The times are simulated.
256 devices in a mesh: dp: 4 (over x), section: 4 (over y_lo, core), mp: 16 (over y_hi, z).
Axes of the slice: x: 4, y: 4 (y_hi: 2, y_lo: 2; y = y_hi * 2 + y_lo), z: 8, core: 2. Of those that a mesh axis runs over, the one named last changes fastest.
Arguments:
- layer_input: bfloat16 [4, 1024, 2048], P('section', 'dp'), may hold values from -6 to 6
- top_grad: bfloat16 [1024, 2048], P('dp'), may hold values from -6 to 6
- norm_gain: float32 [4, 2048], P('section'), may hold values from 0.25 to 1.75
- gate_weight: bfloat16 [4, 2048, 8192], P('section', None, 'mp'), may hold values from -0.125 to 0.125
- up_weight: bfloat16 [4, 2048, 8192], P('section', None, 'mp'), may hold values from -0.125 to 0.125
- down_weight: bfloat16 [4, 8192, 2048], P('section', 'mp'), may hold values from -0.0625 to 0.0625
- first_moment: float32 [4, 2048, 8192], P('section', 'dp', 'mp'), may hold values from -96 to 96
- second_moment: float32 [4, 2048, 8192], P('section', 'dp', 'mp'), may hold values from 16 to 1024
Outputs:
- input_grad: bfloat16 [4, 1024, 2048], P('section', 'dp')
- gate_grad: bfloat16 [4, 2048, 8192], P('section', 'dp', 'mp')
- up_grad: bfloat16 [4, 2048, 8192], P('section', 'dp', 'mp')
- adam_step: float32 [4, 2048, 8192], P('section', 'dp', 'mp')
All inputs are finite; a program needn't handle non-finite values.
Results may differ from a plain program's by a relative error of at most 0.035.
Values may be sent and summed in bfloat16 or wider, within the bound.
A program may use at most 128 MiB of HBM per device.

v0:
```python
import jax
import jax.numpy as jnp
from jax import lax
from jax.sharding import PartitionSpec as P

first_fix = 1.0 - 0.9**20
second_fix = 1.0 - 0.95**20


def passed_along(x, axis, by):
    devices = lax.axis_size(axis)
    pairs = [(i, i + by) for i in range(devices) if 0 <= i + by < devices]
    return lax.ppermute(x, axis, pairs)


def dot_last(left, right):
    return lax.dot_general(
        left, right, (((1,), (1,)), ((), ())), preferred_element_type=jnp.float32
    )


def dot_first(left, right):
    return lax.dot_general(
        left, right, (((0,), (0,)), ((), ())), preferred_element_type=jnp.float32
    )


def on_device(
    layer_input,
    top_grad,
    norm_gain,
    gate_weight,
    up_weight,
    down_weight,
    first_moment,
    second_moment,
):
    section_count = lax.axis_size("section")
    section_place = lax.axis_index("section")
    gate_w = gate_weight[0]
    up_w = up_weight[0]
    down_w = down_weight[0]
    gain_row = norm_gain[0]
    values = layer_input[0].astype(jnp.float32)
    scale_inv = lax.rsqrt(jnp.mean(values * values, axis=-1, keepdims=True) + 1e-05)
    normed = values * scale_inv
    normed_gain = (normed * gain_row).astype(jnp.bfloat16)
    gate_pre = jnp.dot(normed_gain, gate_w, preferred_element_type=jnp.float32)
    up_pre = jnp.dot(normed_gain, up_w, preferred_element_type=jnp.float32)
    sigmoid_gate = jax.nn.sigmoid(gate_pre)
    gated = gate_pre * sigmoid_gate
    hidden = (gated * up_pre).astype(jnp.bfloat16)
    gate_slope = up_pre * sigmoid_gate * (1.0 + gate_pre * (1.0 - sigmoid_gate))
    incoming_grad = top_grad
    saved_grad = jnp.zeros(top_grad.shape, jnp.bfloat16)
    saved_gate = jnp.zeros(hidden.shape, jnp.bfloat16)
    saved_up = jnp.zeros(hidden.shape, jnp.bfloat16)
    saved_sent = jnp.zeros(incoming_grad.shape, jnp.bfloat16)
    for turn_index in range(section_count):
        grad_full = incoming_grad
        grad_hidden = dot_last(grad_full, down_w)
        grad_gate = (grad_hidden * gate_slope).astype(jnp.bfloat16)
        grad_up = (grad_hidden * gated).astype(jnp.bfloat16)
        partial_value = dot_last(grad_gate, gate_w) + dot_last(grad_up, up_w)
        grad_normed = lax.psum(partial_value.astype(jnp.bfloat16), "mp").astype(jnp.float32)
        scaled = grad_normed * gain_row
        projection = jnp.mean(scaled * normed, axis=-1, keepdims=True)
        sent_grad = (
            incoming_grad.astype(jnp.float32) + scale_inv * (scaled - normed * projection)
        ).astype(jnp.bfloat16)
        on_turn = section_place == section_count - 1 - turn_index
        saved_grad = jnp.where(on_turn, grad_full, saved_grad)
        saved_gate = jnp.where(on_turn, grad_gate, saved_gate)
        saved_up = jnp.where(on_turn, grad_up, saved_up)
        saved_sent = jnp.where(on_turn, sent_grad, saved_sent)
        if turn_index + 1 < section_count:
            incoming_grad = passed_along(sent_grad, "section", -1)
    unit_count = gate_w.shape[1]
    summed = lax.psum_scatter(
        jnp.concatenate(
            [
                dot_first(normed_gain, saved_gate),
                dot_first(normed_gain, saved_up),
                dot_first(saved_grad, hidden),
            ],
            axis=1,
        ).astype(jnp.bfloat16),
        "dp",
        scatter_dimension=0,
        tiled=True,
    ).astype(jnp.float32)
    gate_sum = summed[:, :unit_count]
    up_sum = summed[:, unit_count : 2 * unit_count]
    down_sum = summed[:, 2 * unit_count :]
    new_first = 0.9 * first_moment[0] + 0.1 * down_sum
    new_second = 0.95 * second_moment[0] + 0.05 * down_sum * down_sum
    adam_step = new_first / first_fix / (jnp.sqrt(new_second / second_fix) + 1e-08)
    return (
        saved_sent[None],
        gate_sum.astype(jnp.bfloat16)[None],
        up_sum.astype(jnp.bfloat16)[None],
        adam_step[None],
    )


def solution(mesh):
    return jax.shard_map(
        on_device,
        mesh=mesh,
        in_specs=(
            P("section", "dp", None),
            P("dp", None),
            P("section", None),
            P("section", None, "mp"),
            P("section", None, "mp"),
            P("section", "mp", None),
            P("section", "dp", "mp"),
            P("section", "dp", "mp"),
        ),
        out_specs=(
            P("section", "dp", None),
            P("section", "dp", "mp"),
            P("section", "dp", "mp"),
            P("section", "dp", "mp"),
        ),
        check_vma=False,
    )
```

profile of v0, /device:TPU:2, one launch (start us, length us, event | category | flops | bytes accessed | tf_op | source)
XLA Modules:
  0.0 802.3 jit_solution(8956404078611370232)
XLA Ops:
  7.2 1.6 fusion.36
  9.1 2.1 fusion.47
  11.3 0.8 fusion.53
  13.4 1.7 multiply_convert_fusion.8
  15.1 0.7 fusion.45
  15.9 1.7 fusion.11
  17.7 161.6 %all-reduce.5.cloned.1.call-done = bf16[256,2048]{1,0:T(8,128)(2,1)} async-done(((bf16[256,2048]{1,0:T(8,128)(2,1)}), bf16[256,2048]{1,0:T(8,128)(2,1)}) %all-reduce.5.cloned.1.call-update) | async-done | bytes 1048592 | tf_op jit(solution)/shard_map/psum | solution.py:65
  179.3 1.9 fusion.15
  181.3 0.8 fusion.19
  182.1 1.4 collective-permute-start
  183.5 3.3 collective-permute-done
  186.8 0.8 multiply_convert_fusion.5
  187.7 0.7 fusion.43
  188.5 1.0 copy-done.3
  189.5 1.7 fusion.12
  191.3 166.9 %all-reduce.7.cloned.1.call-done = bf16[256,2048]{1,0:T(8,128)(2,1)} async-done(((bf16[256,2048]{1,0:T(8,128)(2,1)}), bf16[256,2048]{1,0:T(8,128)(2,1)}) %all-reduce.7.cloned.1.call-update) | async-done | bytes 1048592 | tf_op jit(solution)/shard_map/psum | solution.py:65
  358.2 1.9 fusion.20
  360.1 0.8 fusion.24
  361.0 1.4 collective-permute-start.1
  362.4 3.3 collective-permute-done.1
  365.7 0.8 multiply_convert_fusion.3
  366.6 0.7 fusion.41
  367.4 1.0 copy-done.4
  368.4 1.7 fusion.13
  370.4 166.6 %all-reduce.9.cloned.1.call-done = bf16[256,2048]{1,0:T(8,128)(2,1)} async-done(((bf16[256,2048]{1,0:T(8,128)(2,1)}), bf16[256,2048]{1,0:T(8,128)(2,1)}) %all-reduce.9.cloned.1.call-update) | async-done | bytes 1048592 | tf_op jit(solution)/shard_map/psum | solution.py:65
  537.0 1.9 fusion.25
  538.9 1.8 fusion.29
  540.7 1.3 collective-permute-start.2
  542.0 3.6 collective-permute-done.2
  545.6 2.9 multiply_convert_fusion.1
  548.5 0.7 fusion.39
  549.3 1.0 copy-done.5
  550.3 1.8 fusion.14
  552.2 2.5 convolution_convert_fusion
  554.8 0.9 convolution_convert_fusion.1
  555.9 0.9 convolution_convert_fusion.2
  556.7 11.3 %pad_maximum_fusion = bf16[2048,1536]{0,1:T(8,128)(2,1)} fusion(bf16[2048,512]{0,1:T(8,128)(2,1)S(1)} %convolution_convert_fusion, bf16[2048,512]{0,1:T(8,128)(2,1)S(1)} %convolution_convert_fusion.1, bf16[2048,512]{0,1:T(8,128)(2,1)S(1)} %convolution_convert_fusion.2), kind=kLoop, calls=%fused_computation | loop fusion | flops 18874368 | bytes 12582912 | tf_op jit(solution)/shard_map/concatenate | solution.py:80
  568.0 2.5 copy.13
  570.6 2.6 copy.12
  573.2 145.6 %all-reduce.11.cloned.1.call-done = bf16[256,2048]{1,0:T(8,128)(2,1)} async-done(((bf16[256,2048]{1,0:T(8,128)(2,1)}), bf16[256,2048]{1,0:T(8,128)(2,1)}) %all-reduce.11.cloned.1.call-update) | async-done | bytes 1048592 | tf_op jit(solution)/shard_map/psum | solution.py:65
  718.8 1.9 fusion.30
  720.7 3.7 fusion.73
  724.5 59.4 %reduce-scatter.2.cloned.1.call-done = bf16[512,1536]{0,1:T(8,128)(2,1)} async-done(((bf16[2048,1536]{0,1:T(8,128)(2,1)}), bf16[512,1536]{0,1:T(8,128)(2,1)}) %reduce-scatter.2.cloned.1.call-update) | async-done | bytes 1572880 | tf_op jit(solution)/shard_map/reduce_scatter | solution.py:79
  783.9 2.2 slice_bitcast_fusion
  786.1 2.0 copy.14
  788.1 2.0 copy.15
  790.2 3.0 fusion.66
  793.2 2.5 copy.16
  (100 shorter events, 2.8 us)
Async XLA Ops:
  7.2 1.9 copy-start
  7.2 172.1 %all-reduce.5.cloned.1.call-start = ((), (), s32[]{:S(2)}) async-start(), calls=%async_computation.1 | async-start | bytes 2097152 | tf_op jit(solution)/shard_map/psum | solution.py:65
  9.1 2.1 copy-start.1
  9.1 2.2 copy-start.2
  9.1 2.2 copy-start.20
  11.3 0.8 copy-start.38
  11.3 1.4 copy-start.14
  11.3 2.1 copy-start.35
  13.4 1.7 copy-start.41
  17.6 340.6 %all-reduce.7.cloned.1.call-start = ((), (), s32[]{:S(2)}) async-start(), calls=%async_computation.2 | async-start | bytes 2097152 | tf_op jit(solution)/shard_map/psum | solution.py:65
  179.3 1.9 copy-start.8
  179.3 1.9 copy-start.15
  181.2 5.5 copy-start.36
  181.3 5.5 copy-start.39
  181.3 5.5 copy-start.42
  182.1 5.5 copy-start.11
  182.1 4.7 collective-permute-start
  186.8 1.0 copy-start.16
  187.7 0.8 copy-start.29
  187.7 1.8 copy-start.3
  191.3 345.7 %all-reduce.9.cloned.1.call-start = ((), (), s32[]{:S(2)}) async-start(), calls=%async_computation.3 | async-start | bytes 2097152 | tf_op jit(solution)/shard_map/psum | solution.py:65
  358.2 1.9 copy-start.9
  358.2 1.9 copy-start.17
  360.1 5.5 copy-start.37
  360.1 5.5 copy-start.40
  360.1 5.5 copy-start.43
  360.9 5.5 copy-start.13
  361.0 4.7 collective-permute-start.1
  365.6 1.0 copy-start.18
  366.6 0.8 copy-start.31
  366.6 1.8 copy-start.4
  370.1 348.6 %all-reduce.11.cloned.1.call-start = ((), (), s32[]{:S(2)}) async-start(), calls=%async_computation.4 | async-start | bytes 2097152 | tf_op jit(solution)/shard_map/psum | solution.py:65
  537.0 1.9 copy-start.10
  537.0 1.9 copy-start.19
  540.7 4.9 collective-permute-start.2
  548.5 0.8 copy-start.25
  548.5 1.8 copy-start.5
  552.1 231.8 %reduce-scatter.2.cloned.1.call-start = ((), (), s32[]{:S(2)}) async-start(), calls=%async_computation.5 | async-start | bytes 7864320 | tf_op jit(solution)/shard_map/reduce_scatter | solution.py:79
  552.1 2.6 copy-start.28
  552.2 2.6 copy-start.30
  552.2 2.6 copy-start.32
  552.2 2.6 copy-start.34
  554.7 1.0 copy-start.22
  554.8 1.0 copy-start.24
  554.8 1.1 copy-start.26
  718.8 1.9 copy-start.7
  718.8 1.9 copy-start.12
  724.5 65.7 %copy-start.6 = (f32[1,512,512]{1,2,0:T(8,128)S(1)}, f32[1,512,512]{1,2,0:T(8,128)}, u32[]{:S(2)}) copy-start(f32[1,512,512]{1,2,0:T(8,128)} %copy.13) | copy-start | bytes 3145732
  (4 other events, 3.0 us)
Sparse Core Ops, SparseCore 0:
  17.7 161.5 all-reduce.4
  191.4 166.7 all-reduce.6
  370.3 166.6 all-reduce.8
  552.2 166.5 all-reduce.10
  721.2 62.6 reduce-scatter.1
where the time goes:
time: 805 us; the launch traced here: 802 us
  waiting for transfers between devices  710 us (88%)
  other arithmetic  30.8 us (4%)
  matrix products  23.2 us (3%)
  local copies, waits for them, and re-layouts  19.3 us (2%)
  between operations  14.3 us (2%)
    psum x4, waiting for transfers between devices, on_device(): lax.psum(partial_value.astype(jnp.bfloat16), 'mp').astype(jnp.float32)  641 us
    reduce_scatter x1, waiting for transfers between devices, on_device(): lax.psum_scatter(jnp.concatenate([dot_first(normed_gain, saved_gate), dot...  59.4 us
    unnamed x93, local copies, waits for them, and re-layouts  17 us
  transfers between devices with their start and end apart: 8, of which 8 were waited for; matrix products, arithmetic and copies ran while one was open for 3% of the time, Pallas kernels for 0%

commit v1 on v0

v1 whole, which is shorter than its diff:
```python
import jax
import jax.numpy as jnp
from jax import lax
from jax.experimental import pallas as pl
from jax.experimental.pallas import tpu as pltpu
from jax.sharding import PartitionSpec as P

first_fix = 1.0 - 0.9**20
second_fix = 1.0 - 0.95**20

MESH = pl.DeviceIdType.MESH
F32 = jnp.float32
BF16 = jnp.bfloat16

ROWS = 256
D = 2048
UNITS = 512
HALF = D // 2
CHUNKS = 4
CH = ROWS // CHUNKS
BLOCKS = CH // 8
FAR_FIRST = (4, 3, 5, 2, 6, 1, 7, 0)


def dot_nn(left, right):
    return lax.dot_general(left, right, (((1,), (0,)), ((), ())), preferred_element_type=F32)


def dot_nt(left, right):
    return lax.dot_general(left, right, (((1,), (1,)), ((), ())), preferred_element_type=F32)


def kernel(
    li_h, tg_h, gain_h, gw_h, uw_h, dw_h, fm_h, sm_h,
    ig_o, gg_o, ug_o, ad_o,
    li, w, dw, up, gain, fm, sm,
    ng, gated, slope, gx, hx, ngx, ux, ngt, uxt,
    snd, rsbuf, rout, agbuf, igbuf, ig, gg, ug, ad,
    liown, gnown, incb, tgown,
    ld, rs_r, ag_r, ig_r, li_r, gn_r, inc_r, dp_r,
    rs_s, ag_s, inc_s, li_s, gn_s, fw_s, dp_s, own_s, out_s,
):
    d = lax.axis_index("dp")
    s = lax.axis_index("section")
    m = lax.axis_index("mp")
    yh, z = m // 8, m % 8
    owner = jnp.where(s >= 2, 0, 3)
    turn = 1 - s % 2

    def local(src, dst, sem):
        return pltpu.make_async_copy(src, dst, sem)

    def remote(src, dst, ssem, rsem, **to):
        return pltpu.make_async_remote_copy(src, dst, ssem, rsem, device_id=to, device_id_type=MESH)

    loads = [
        local(li_h.at[0], li, ld.at[0]),
        local(gain_h, gain, ld.at[1]),
        local(gw_h.at[0], w.at[:, pl.ds(0, UNITS)], ld.at[2]),
        local(uw_h.at[0], w.at[:, pl.ds(UNITS, UNITS)], ld.at[3]),
        local(dw_h.at[0], dw, ld.at[4]),
    ]
    late = [local(fm_h.at[0], fm, ld.at[5]), local(sm_h.at[0], sm, ld.at[6])]
    tg_load = local(tg_h, up, ld.at[7])

    def block16(i):
        return pl.ds(pl.multiple_of(CH * (yh + 2 * i) + 16 * (z // 2), 16), 16)

    tg_rows = [local(tg_h.at[block16(i)], tgown.at[i], ld.at[8 + i]) for i in range(2)]

    for cp in loads:
        cp.start()

    @pl.when(s == 3)
    def _():
        tg_load.start()

    @pl.when(s == 0)
    def _():
        for cp in tg_rows:
            cp.start()

    for cp in late:
        cp.start()

    loads[0].wait()
    loads[1].wait()
    li_sends = [
        remote(li.at[block16(i)], liown.at[turn, i], li_s.at[i], li_r.at[turn, i], section=owner)
        for i in range(2)
    ]
    gn_send = remote(gain, gnown.at[turn], gn_s.at[0], gn_r.at[turn], section=owner)
    for cp in li_sends:
        cp.start()
    gn_send.start()

    def norm_rows(j, carry):
        rows = pl.ds(pl.multiple_of(j * 32, 32), 32)
        values = li[rows, :].astype(F32)
        scale_inv = lax.rsqrt(jnp.mean(values * values, axis=-1, keepdims=True) + 1e-05)
        ng[rows, :] = (values * scale_inv * gain[...]).astype(BF16)
        return carry

    lax.fori_loop(0, ROWS // 32, norm_rows, 0)
    loads[2].wait()
    loads[3].wait()

    def forward(j, carry):
        cols = pl.ds(pl.multiple_of(j * 256, 256), 256)
        cols_up = pl.ds(pl.multiple_of(UNITS + j * 256, 256), 256)
        gate_pre = dot_nn(ng[...], w[:, cols])
        up_pre = dot_nn(ng[...], w[:, cols_up])
        sig = jax.nn.sigmoid(gate_pre)
        gate = gate_pre * sig
        gated[:, cols] = gate
        hx[0, :, cols] = (gate * up_pre).astype(BF16)
        slope[:, cols] = up_pre * sig * (1.0 + gate_pre * (1.0 - sig))
        return carry

    lax.fori_loop(0, UNITS // 256, forward, 0)
    loads[4].wait()

    def feature_cols(k):
        return pl.ds(pl.multiple_of(lax.rem(d + k, 4) * 512, 512), 512)

    own_ng = local(ng.at[:, feature_cols(0)], ngx.at[0], own_s.at[0])

    def bulk():
        own_ng.start()
        for k in (2, 1, 3):
            peer = lax.rem(d + k, 4)
            remote(ng.at[:, feature_cols(k)], ngx.at[4 - k], dp_s.at[0], dp_r.at[0], dp=peer).start()
            remote(hx.at[0], hx.at[4 - k], dp_s.at[1], dp_r.at[1], dp=peer).start()

    def reduce_layer(u, i, incoming, sends):
        remote(rsbuf.at[u, i], rsbuf.at[u, i], rs_s.at[0], rs_r.at[u, i], mp=m).wait_recv()
        even = z % 2 == 0
        values = liown[u, i].astype(F32)
        values = jnp.where(even, values[:8], values[8:])
        scale_inv = lax.rsqrt(jnp.mean(values * values, axis=-1, keepdims=True) + 1e-05)
        normed = values * scale_inv
        total = rsbuf[u, i, 0].astype(F32)
        for k in range(1, 16):
            total = total + rsbuf[u, i, k].astype(F32)
        scaled_l = total[:8] * gnown[u, :, pl.ds(0, HALF)]
        scaled_r = total[8:] * gnown[u, :, pl.ds(HALF, HALF)]
        norm_l, norm_r = normed[:, :HALF], normed[:, HALF:]
        both = jnp.sum(scaled_l * norm_l + scaled_r * norm_r, axis=-1, keepdims=True)
        projection = both * (1.0 / D)
        inc_l, inc_r = incoming(i)
        out_l = inc_l + scale_inv * (scaled_l - norm_l * projection)
        out_r = inc_r + scale_inv * (scaled_r - norm_r * projection)
        rout[u, i] = jnp.concatenate([out_l, out_r], axis=0).astype(BF16)
        sends(u, i)

    def halves(block):
        block = block.astype(F32)
        return block[:8], block[8:]

    def gather_to(section, buf, sem):
        def sends(u, i):
            chunk = yh + 2 * i
            for k in FAR_FIRST:
                for h in range(2):
                    to = lax.rem(z + k, 8) + 8 * h
                    remote(
                        rout.at[u, i], buf.at[chunk, z], ag_s.at[u, i], sem.at[chunk], section=section, mp=to
                    ).start()
        return sends

    def own_rows_ready(u):
        for i in range(2):
            remote(liown.at[u, i], liown.at[u, i], li_s.at[0], li_r.at[u, i], mp=m).wait_recv()
        remote(gnown.at[u], gnown.at[u], gn_s.at[0], gn_r.at[u], mp=m).wait_recv()

    def from_rout(i):
        return halves(rout[0, i])

    def wait_gather_sends():
        for u in range(2):
            for i in range(2):
                remote(rsbuf.at[u, i], rsbuf.at[u, i], ag_s.at[u, i], rs_r.at[u, i], mp=m).wait_send()

    @pl.when(s < 3)
    def _():
        bulk()

    @pl.when(s == 0)
    def _():
        for cp in tg_rows:
            cp.wait()
        own_rows_ready(0)
        own_rows_ready(1)

        def from_top(i):
            block = tgown[i].astype(F32)
            rows = jnp.where(z % 2 == 0, block[:8], block[8:])
            return rows[:, :HALF], rows[:, HALF:]

        def sends_two(u, i):
            gather_to(1, agbuf, ag_r)(u, i)
            remote(rout.at[u, i], incb.at[i], inc_s.at[i], inc_r.at[i], section=3).start()

        for i in range(2):
            reduce_layer(0, i, from_top, gather_to(2, agbuf, ag_r))
        for i in range(2):
            reduce_layer(1, i, from_rout, sends_two)

    @pl.when(s == 3)
    def _():
        tg_load.wait()

    below = jnp.where(s == 3, 0, s + 1)

    def unpack(src, c, dst):
        def pair(j, carry):
            a_l, a_r = halves(src[c, 2 * j])
            b_l, b_r = halves(src[c, 2 * j + 1])
            rows = pl.ds(pl.multiple_of(CH * c + 16 * j, 16), 16)
            dst[rows, pl.ds(0, HALF)] = jnp.concatenate([a_l, b_l], axis=0).astype(BF16)
            dst[rows, pl.ds(HALF, HALF)] = jnp.concatenate([a_r, b_r], axis=0).astype(BF16)
            return carry
        lax.fori_loop(0, BLOCKS // 2, pair, 0)

    def chunk_step(c, carry):
        rows = pl.ds(pl.multiple_of(CH * c, CH), CH)

        @pl.when(s < 3)
        def _():
            remote(agbuf.at[c], agbuf.at[c], rs_s.at[0], ag_r.at[c], mp=m).wait_recv()
            unpack(agbuf, c, up)

        grad_hidden = dot_nt(up[rows, :], dw[...])
        gx[0, rows, pl.ds(0, UNITS)] = (grad_hidden * slope[rows, :]).astype(BF16)
        gx[0, rows, pl.ds(UNITS, UNITS)] = (grad_hidden * gated[rows, :]).astype(BF16)

        def tile(t, carry):
            cols = pl.ds(pl.multiple_of(t * 512, 512), 512)
            cols_right = pl.ds(pl.multiple_of(HALF + t * 512, 512), 512)
            left = dot_nt(gx[0, rows, :], w[cols, :])
            right = dot_nt(gx[0, rows, :], w[cols_right, :])
            for b in range(BLOCKS):
                both = jnp.concatenate([left[8 * b : 8 * b + 8], right[8 * b : 8 * b + 8]], axis=0)
                snd[c, b, :, cols] = both.astype(BF16)
            return carry

        lax.fori_loop(0, 2, tile, 0)
        for k in FAR_FIRST:
            to = lax.rem(z + k, 8)
            remote(
                snd.at[c, to], rsbuf.at[turn, c // 2, m], rs_s.at[0], rs_r.at[turn, c // 2],
                section=owner, mp=to + 8 * (c % 2),
            ).start()

        @pl.when(s < 3)
        def _():
            remote(agbuf.at[c], igbuf.at[c], fw_s.at[0], ig_r.at[c], section=below).start()

        local(up.at[rows, feature_cols(0)], ux.at[0, rows], own_s.at[1]).start()
        for k in (2, 1, 3):
            peer = lax.rem(d + k, 4)
            remote(gx.at[0, rows], gx.at[4 - k, rows], dp_s.at[2], dp_r.at[2], dp=peer).start()
            remote(up.at[rows, feature_cols(k)], ux.at[4 - k, rows], dp_s.at[3], dp_r.at[3], dp=peer).start()
        return carry

    lax.fori_loop(0, CHUNKS, chunk_step, 0)

    @pl.when(s == 3)
    def _():
        bulk()
        own_rows_ready(0)
        own_rows_ready(1)
        for i in range(2):
            remote(incb.at[i], incb.at[i], inc_s.at[0], inc_r.at[i], mp=m).wait_recv()

        def from_inc(i):
            return halves(incb[i])

        for i in range(2):
            reduce_layer(0, i, from_inc, gather_to(0, agbuf, ag_r))
        for i in range(2):
            reduce_layer(1, i, from_rout, gather_to(0, igbuf, ig_r))

    others = pl.ds(1, 3)
    for cp in late:
        cp.wait()
    own_ng.wait()
    local(ux.at[0], ux.at[0], own_s.at[1]).wait()
    remote(ngx.at[others], ngx.at[others], dp_s.at[0], dp_r.at[0], mp=m).wait_recv()
    remote(hx.at[others], hx.at[others], dp_s.at[1], dp_r.at[1], mp=m).wait_recv()
    for k in range(4):
        ngt[:, pl.ds(ROWS * k, ROWS)] = ngx[k].T
    remote(ux.at[others], ux.at[others], dp_s.at[3], dp_r.at[3], mp=m).wait_recv()
    for k in range(4):
        uxt[:, pl.ds(ROWS * k, ROWS)] = ux[k].T

    def down_tile(j, carry):
        cols = pl.ds(pl.multiple_of(j * 256, 256), 256)
        hidden = hx[:, :, cols].reshape(4 * ROWS, 256)
        down_sum = dot_nn(uxt[...], hidden)
        new_first = 0.9 * fm[:, cols] + 0.1 * down_sum
        new_second = 0.95 * sm[:, cols] + 0.05 * down_sum * down_sum
        ad[:, cols] = new_first / first_fix / (jnp.sqrt(new_second / second_fix) + 1e-08)
        return carry

    lax.fori_loop(0, UNITS // 256, down_tile, 0)
    ad_out = local(ad, ad_o.at[0], out_s.at[0])
    ad_out.start()
    remote(gx.at[others], gx.at[others], dp_s.at[2], dp_r.at[2], mp=m).wait_recv()

    def grad_tile(j, carry):
        cols = pl.ds(pl.multiple_of(j * 256, 256), 256)
        cols_up = pl.ds(pl.multiple_of(UNITS + j * 256, 256), 256)
        gate = gx[:, :, cols].reshape(4 * ROWS, 256)
        gg[:, cols] = dot_nn(ngt[...], gate).astype(BF16)
        upg = gx[:, :, cols_up].reshape(4 * ROWS, 256)
        ug[:, cols] = dot_nn(ngt[...], upg).astype(BF16)
        return carry

    lax.fori_loop(0, UNITS // 256, grad_tile, 0)
    gg_out = local(gg, gg_o.at[0], out_s.at[1])
    ug_out = local(ug, ug_o.at[0], out_s.at[2])
    gg_out.start()
    ug_out.start()

    def last_chunk(c, carry):
        remote(igbuf.at[c], igbuf.at[c], rs_s.at[0], ig_r.at[c], mp=m).wait_recv()
        unpack(igbuf, c, ig)
        rows = pl.ds(pl.multiple_of(CH * c, CH), CH)
        local(ig.at[rows], ig_o.at[0, rows], out_s.at[3]).start()
        return carry

    lax.fori_loop(0, CHUNKS, last_chunk, 0)

    for cp in li_sends:
        cp.wait_send()
    gn_send.wait_send()
    remote(snd, snd, rs_s.at[0], rs_r.at[0, 0], mp=m).wait_send()
    remote(ngx.at[others], ngx.at[others], dp_s.at[0], dp_r.at[0], mp=m).wait_send()
    remote(hx.at[others], hx.at[others], dp_s.at[1], dp_r.at[1], mp=m).wait_send()
    remote(gx.at[others], gx.at[others], dp_s.at[2], dp_r.at[2], mp=m).wait_send()
    remote(ux.at[others], ux.at[others], dp_s.at[3], dp_r.at[3], mp=m).wait_send()

    @pl.when(s < 3)
    def _():
        remote(agbuf, agbuf, fw_s.at[0], ag_r.at[0], mp=m).wait_send()

    @pl.when(s == 0)
    def _():
        wait_gather_sends()
        for i in range(2):
            remote(rout.at[1, i], incb.at[i], inc_s.at[i], inc_r.at[i], mp=m).wait_send()

    @pl.when(s == 3)
    def _():
        wait_gather_sends()

    ad_out.wait()
    gg_out.wait()
    ug_out.wait()
    local(ig, ig_o.at[0], out_s.at[3]).wait()


def on_device(layer_input, top_grad, norm_gain, gate_weight, up_weight, down_weight, first_moment, second_moment):
    V, DMA = pltpu.VMEM, pltpu.SemaphoreType.DMA
    pieces = (16, HALF)
    return pl.pallas_call(
        kernel,
        out_shape=(
            jax.ShapeDtypeStruct((1, ROWS, D), BF16),
            jax.ShapeDtypeStruct((1, 512, UNITS), BF16),
            jax.ShapeDtypeStruct((1, 512, UNITS), BF16),
            jax.ShapeDtypeStruct((1, 512, UNITS), F32),
        ),
        in_specs=[pl.BlockSpec(memory_space=pl.ANY)] * 8,
        out_specs=[pl.BlockSpec(memory_space=pl.ANY)] * 4,
        scratch_shapes=[
            V((ROWS, D), BF16),
            V((D, 2 * UNITS), BF16),
            V((UNITS, D), BF16),
            V((ROWS, D), BF16),
            V((1, D), F32),
            V((512, UNITS), F32),
            V((512, UNITS), F32),
            V((ROWS, D), BF16),
            V((ROWS, UNITS), F32),
            V((ROWS, UNITS), F32),
            V((4, ROWS, 2 * UNITS), BF16),
            V((4, ROWS, UNITS), BF16),
            V((4, ROWS, 512), BF16),
            V((4, ROWS, 512), BF16),
            V((512, 4 * ROWS), BF16),
            V((512, 4 * ROWS), BF16),
            V((CHUNKS, BLOCKS) + pieces, BF16),
            V((2, 2, 16) + pieces, BF16),
            V((2, 2) + pieces, BF16),
            V((CHUNKS, BLOCKS) + pieces, BF16),
            V((CHUNKS, BLOCKS) + pieces, BF16),
            V((ROWS, D), BF16),
            V((512, UNITS), BF16),
            V((512, UNITS), BF16),
            V((512, UNITS), F32),
            V((2, 2, 16, D), BF16),
            V((2, 1, D), F32),
            V((2,) + pieces, BF16),
            V((2, 16, D), BF16),
            DMA((10,)),
            DMA((2, 2)),
            DMA((CHUNKS,)),
            DMA((CHUNKS,)),
            DMA((2, 2)),
            DMA((2,)),
            DMA((2,)),
            DMA((4,)),
            DMA((1,)),
            DMA((2, 2)),
            DMA((2,)),
            DMA((2,)),
            DMA((1,)),
            DMA((1,)),
            DMA((4,)),
            DMA((2,)),
            DMA((4,)),
        ],
        compiler_params=pltpu.CompilerParams(has_side_effects=True, vmem_limit_bytes=50 * 1024 * 1024),
        name="relay",
    )(layer_input, top_grad, norm_gain, gate_weight, up_weight, down_weight, first_moment, second_moment)


def solution(mesh):
    return jax.shard_map(
        on_device,
        mesh=mesh,
        in_specs=(
            P("section", "dp", None),
            P("dp", None),
            P("section", None),
            P("section", None, "mp"),
            P("section", None, "mp"),
            P("section", "mp", None),
            P("section", "dp", "mp"),
            P("section", "dp", "mp"),
        ),
        out_specs=(
            P("section", "dp", None),
            P("section", "dp", "mp"),
            P("section", "dp", "mp"),
            P("section", "dp", "mp"),
        ),
        check_vma=False,
    )
```

time: 805 us -> 112 us (0.14)
  waiting for transfers between devices: 710 us -> 0 us
  Pallas kernels: 0 us -> 107 us
  other arithmetic: 30.8 us -> 0 us
  matrix products: 23.2 us -> 0 us
  local copies, waits for them, and re-layouts: 19.3 us -> 4.22 us
  between operations: 14.3 us -> 0.65 us
    psum x4 -> x0, waiting for transfers between devices: 641 us -> none  [on_device(): lax.psum(partial_value.astype(jnp.bfloat16), 'mp').astype(jnp.float32)]
    pallas_call x0 -> x1, Pallas kernels: none -> 107 us  [on_device(): pl.pallas_call(kernel, out_shape=(jax.ShapeDtypeStruct((1, ROWS, D), BF16...]
    reduce_scatter x1 -> x0, waiting for transfers between devices: 59.4 us -> none  [on_device(): lax.psum_scatter(jnp.concatenate([dot_first(normed_gain, saved_gate), dot...]
    dot_general x17 -> x0, matrix products: 23.2 us -> none  [the longest x12 16.1 us: dot_last(): lax.dot_general(left, right, (((1,), (1,)), ((), ())), preferred_element_...]
    unnamed x93 -> x6, local copies, waits for them, and re-layouts: 17 us -> 4.22 us
    concatenate x1 -> x0, other arithmetic: 11.3 us -> none  [on_device(): jnp.concatenate([dot_first(normed_gain, saved_gate), dot_first(normed_gai...]
    ppermute x3 -> x0, waiting for transfers between devices: 10.1 us -> none  [passed_along(): return lax.ppermute(x, axis, pairs)]
    reduce_sum x5 -> x0, other arithmetic: 9.32 us -> none  [the longest x4 7.67 us: on_device(): projection = jnp.mean(scaled * normed, axis=-1, keepdims=True)]
  transfers between devices with their start and end apart: 8 -> 0, of which waited for: 8 -> 0; matrix products, arithmetic and copies ran while one was open for 3% -> 0% of each run, Pallas kernels for 0% -> 0%
where the time goes in v1:
time: 112 us
  Pallas kernels  107 us (96%)
  local copies, waits for them, and re-layouts  4.22 us (4%)
    pallas_call x1, Pallas kernels, on_device(): pl.pallas_call(kernel, out_shape=(jax.ShapeDtypeStruct((1, ROWS, D), BF16...  107 us
    unnamed x6, local copies, waits for them, and re-layouts  4.22 us

profile of v1, /device:TPU:2, one launch (start us, length us, event | category | flops | bytes accessed | tf_op | source)
XLA Modules:
  0.0 112.3 jit_solution(17595128176879165592)
XLA Ops:
  0.6 0.0 copy-start
  0.6 0.7 copy-done
  1.3 107.5 %relay.1 = (bf16[1,256,2048]{2,1,0:T(8,128)(2,1)S(1)}, bf16[1,512,512]{2,1,0:T(8,128)(2,1)S(1)}, bf16[1,512,512]{2,1,0:T(8,128)(2,1)S(1)}, f32[1,512,512]{2,1,0:T(8,128)S(1)}) custom-call(bf16[1,256,2048]{2,1,0:T(8,128)(2,1)} %li_h.1, bf16[256,2048]{1,0:T(8,128)(2,1)} %tg_h.1, f32[1,2048]{1,0:T(1,128)S(1)} %copy-done, bf16[1,2048,512]{2,1,0:T(8,128)(2,1)} %gw_h.1, ...), custom_call_target="tpu_custom_call" | custom-call | tf_op jit(solution)/shard_map/relay/pallas_call | solution.py:367
  108.8 1.0 copy.16
  109.8 0.8 copy.17
  110.6 0.8 copy.18
  111.4 1.0 copy.19
Async XLA Ops:
  0.6 0.7 copy-start

commit v2 on v1

v2 whole, which is shorter than its diff:
```python
import jax
import jax.numpy as jnp
from jax import lax
from jax.experimental import pallas as pl
from jax.experimental.pallas import tpu as pltpu
from jax.sharding import PartitionSpec as P

first_fix = 1.0 - 0.9**20
second_fix = 1.0 - 0.95**20

MESH = pl.DeviceIdType.MESH
F32 = jnp.float32
BF16 = jnp.bfloat16

ROWS = 256
D = 2048
UNITS = 512
QUARTER = D // 4
CHUNKS = 8
CH = ROWS // CHUNKS
BLOCKS = CH // 4
TURNS = CHUNKS // 2
FAR_FIRST = (4, 3, 5, 2, 6, 1, 7, 0)


def dot_nn(left, right):
    return lax.dot_general(left, right, (((1,), (0,)), ((), ())), preferred_element_type=F32)


def dot_nt(left, right):
    return lax.dot_general(left, right, (((1,), (1,)), ((), ())), preferred_element_type=F32)


def swap(a, b):
    low = lax.broadcasted_iota(jnp.int32, a.shape, 0) < 4
    first = jnp.where(low, a, pltpu.roll(b, 4, 0))
    second = jnp.where(low, pltpu.roll(a, 4, 0), b)
    return first, second


def pack(quarters):
    a_top, b_top = swap(quarters[0], quarters[1])
    a_low, b_low = swap(quarters[2], quarters[3])
    return jnp.concatenate([a_top, a_low], axis=0), jnp.concatenate([b_top, b_low], axis=0)


def unpack_pair(a, b):
    first = swap(a[:8], b[:8])
    second = swap(a[8:], b[8:])
    return first + second


def row_sums(packed):
    folded = packed[:8] + packed[8:]
    folded = folded + pltpu.roll(folded, 4, 0)
    sums = jnp.sum(folded, axis=-1, keepdims=True)
    return jnp.concatenate([sums, sums], axis=0)


def quarters_of(rows):
    return [rows[:, QUARTER * q : QUARTER * (q + 1)] for q in range(4)]


def kernel(
    li_h, tg_h, gain_h, gw_h, uw_h, dw_h, fm_h, sm_h,
    ig, gg, ug, ad,
    li, w, dw, wt, dwt, up, gain, fm, sm,
    ng, gated, slope, gx, hx, ngx, ux, ngt, uxt,
    snd, rsbuf, rout, agbuf, igbuf,
    lisend, liown, gnown, incb, tgown,
    ld, rs_r, ag_r, ig_r, li_r, gn_r, inc_r, dp_r,
    rs_s, ag_s, inc_s, li_s, gn_s, fw_s, dp_s, own_s,
):
    d = lax.axis_index("dp")
    s = lax.axis_index("section")
    m = lax.axis_index("mp")
    yh, z = m // 8, m % 8
    owner = jnp.where(s >= 2, 0, 3)
    turn = 1 - s % 2

    def local(src, dst, sem):
        return pltpu.make_async_copy(src, dst, sem)

    def remote(src, dst, ssem, rsem, **to):
        return pltpu.make_async_remote_copy(src, dst, ssem, rsem, device_id=to, device_id_type=MESH)

    li_load = local(li_h.at[0], li, ld.at[0])
    gain_load = local(gain_h, gain, ld.at[1])
    gw_load = local(gw_h.at[0], w.at[:, pl.ds(0, UNITS)], ld.at[2])
    uw_load = local(uw_h.at[0], w.at[:, pl.ds(UNITS, UNITS)], ld.at[3])
    dw_load = local(dw_h.at[0], dw, ld.at[4])
    late = [local(fm_h.at[0], fm, ld.at[5]), local(sm_h.at[0], sm, ld.at[6])]
    tg_load = local(tg_h, up, ld.at[7])

    def own_tile(i):
        return pl.ds(pl.multiple_of(CH * (yh + 2 * i) + 16 * (z // 4), 16), 16)

    tg_rows = [local(tg_h.at[own_tile(i)], tgown.at[i], ld.at[8 + i]) for i in range(TURNS)]

    li_load.start()
    gain_load.start()

    @pl.when(s == 3)
    def _():
        tg_load.start()

    gw_load.start()
    uw_load.start()
    dw_load.start()

    @pl.when(s == 0)
    def _():
        for cp in tg_rows:
            cp.start()

    for cp in late:
        cp.start()

    barrier = pltpu.get_barrier_semaphore()

    def greet(**to):
        pl.semaphore_signal(barrier, inc=1, device_id=to, device_id_type=MESH)

    def greet_all(section):
        def one(j, carry):
            greet(section=section, mp=j)
            return carry
        lax.fori_loop(0, 16, one, 0)

    for k in (1, 2, 3):
        greet(dp=lax.rem(d + k, 4))

    @pl.when(s == 3)
    def _():
        greet_all(0)
        greet_all(1)
        greet(section=2)

    @pl.when(s == 2)
    def _():
        greet_all(0)
        greet(section=1)

    @pl.when(s == 1)
    def _():
        greet_all(0)

    @pl.when(s == 0)
    def _():
        greet_all(3)
        greet_all(2)

    def own_piece(tile):
        tile = tile.astype(F32)
        rows = jnp.where((z // 2) % 2 == 0, tile[:8], tile[8:])
        a, b = pack(quarters_of(rows))
        return jnp.where(z % 2 == 0, a, b)

    li_load.wait()
    gain_load.wait()
    for i in range(TURNS):
        lisend[i] = own_piece(li[own_tile(i), :]).astype(BF16)
    li_send = remote(lisend, liown.at[turn], li_s.at[0], li_r.at[turn], section=owner)
    gn_send = remote(gain, gnown.at[turn], gn_s.at[0], gn_r.at[turn], section=owner)

    def norm_rows(j, carry):
        rows = pl.ds(pl.multiple_of(j * 32, 32), 32)
        values = li[rows, :].astype(F32)
        scale_inv = lax.rsqrt(jnp.mean(values * values, axis=-1, keepdims=True) + 1e-05)
        ng[rows, :] = (values * scale_inv * gain[...]).astype(BF16)
        return carry

    lax.fori_loop(0, ROWS // 32, norm_rows, 0)
    gw_load.wait()
    uw_load.wait()

    def forward(j, carry):
        cols = pl.ds(pl.multiple_of(j * 256, 256), 256)
        cols_up = pl.ds(pl.multiple_of(UNITS + j * 256, 256), 256)
        gate_pre = dot_nn(ng[...], w[:, cols])
        up_pre = dot_nn(ng[...], w[:, cols_up])
        sig = jax.nn.sigmoid(gate_pre)
        gate = gate_pre * sig
        gated[:, cols] = gate
        hx[0, :, cols] = (gate * up_pre).astype(BF16)
        slope[:, cols] = up_pre * sig * (1.0 + gate_pre * (1.0 - sig))
        return carry

    lax.fori_loop(0, UNITS // 256, forward, 0)

    @pl.when(s == 3)
    def _():
        pl.semaphore_wait(barrier, 19)

    @pl.when((s == 2) | (s == 1))
    def _():
        pl.semaphore_wait(barrier, 20)

    @pl.when(s == 0)
    def _():
        pl.semaphore_wait(barrier, 51)

    li_send.start()
    gn_send.start()
    dw_load.wait()

    def feature_cols(k):
        return pl.ds(pl.multiple_of(lax.rem(d + k, 4) * 512, 512), 512)

    own_ng = local(ng.at[:, feature_cols(0)], ngx.at[0], own_s.at[0])

    def bulk():
        own_ng.start()
        for k in (2, 1, 3):
            peer = lax.rem(d + k, 4)
            remote(ng.at[:, feature_cols(k)], ngx.at[4 - k], dp_s.at[0], dp_r.at[0], dp=peer).start()
            remote(hx.at[0], hx.at[4 - k], dp_s.at[1], dp_r.at[1], dp=peer).start()

    def reduce_layer(u, incoming, sends):
        def chunk(i, carry):
            remote(rsbuf.at[u, i], rsbuf.at[u, i], rs_s.at[0], rs_r.at[u, i], mp=m).wait_recv()
            values = liown[u, i].astype(F32)
            scale_inv = lax.rsqrt(row_sums(values * values) * (1.0 / D) + 1e-05)
            normed = values * scale_inv
            total = rsbuf[u, i, 0].astype(F32)
            for k in range(1, 16):
                total = total + rsbuf[u, i, k].astype(F32)
            quarter = lax.broadcasted_iota(jnp.int32, (16, QUARTER), 0) // 4
            gain_piece = jnp.zeros((16, QUARTER), F32)
            for q in range(4):
                gain_piece = jnp.where(quarter == q, gnown[u, :, pl.ds(QUARTER * q, QUARTER)], gain_piece)
            scaled = total * gain_piece
            projection = row_sums(scaled * normed) * (1.0 / D)
            rout[u, i] = (incoming(i) + scale_inv * (scaled - normed * projection)).astype(BF16)
            sends(u, i)
            return carry

        lax.fori_loop(0, TURNS, chunk, 0)

    def gather_to(section, buf, sem):
        def sends(u, i):
            chunk = yh + 2 * i
            for k in FAR_FIRST:
                for h in range(2):
                    to = lax.rem(z + k, 8) + 8 * h
                    remote(
                        rout.at[u, i], buf.at[chunk, z], ag_s.at[u], sem.at[chunk], section=section, mp=to
                    ).start()
        return sends

    def own_rows_ready(u):
        remote(liown.at[u], liown.at[u], li_s.at[0], li_r.at[u], mp=m).wait_recv()
        remote(gnown.at[u], gnown.at[u], gn_s.at[0], gn_r.at[u], mp=m).wait_recv()

    def from_rout(i):
        return rout[0, i].astype(F32)

    def wait_gather_sends():
        for u in range(2):
            remote(rsbuf.at[u], rsbuf.at[u], ag_s.at[u], rs_r.at[u, 0], mp=m).wait_send()

    @pl.when(s < 3)
    def _():
        bulk()

        def turn_w(j, carry):
            rows = pl.ds(pl.multiple_of(j * 256, 256), 256)
            wt[:, rows] = w[rows, :].T
            return carry

        lax.fori_loop(0, D // 256, turn_w, 0)

        def turn_dw(j, carry):
            rows = pl.ds(pl.multiple_of(j * 256, 256), 256)
            dwt[:, rows] = dw[rows, :].T
            return carry

        lax.fori_loop(0, UNITS // 256, turn_dw, 0)

    @pl.when(s == 0)
    def _():
        for cp in tg_rows:
            cp.wait()
        own_rows_ready(0)
        own_rows_ready(1)

        def from_top(i):
            return own_piece(tgown[i])

        def sends_two(u, i):
            gather_to(1, agbuf, ag_r)(u, i)
            remote(rout.at[u, i], incb.at[i], inc_s.at[0], inc_r.at[i], section=3).start()

        reduce_layer(0, from_top, gather_to(2, agbuf, ag_r))
        reduce_layer(1, from_rout, sends_two)

    below = jnp.where(s == 3, 0, s + 1)

    def unpack(src, c, dst):
        for p in range(2):
            rows = pl.ds(pl.multiple_of(CH * c + 16 * p, 16), 16)
            top = unpack_pair(src[c, 4 * p].astype(F32), src[c, 4 * p + 1].astype(F32))
            low = unpack_pair(src[c, 4 * p + 2].astype(F32), src[c, 4 * p + 3].astype(F32))
            for q in range(4):
                both = jnp.concatenate([top[q], low[q]], axis=0)
                dst[rows, pl.ds(QUARTER * q, QUARTER)] = both.astype(BF16)

    def send_partials(c, product):
        for t in range(2):
            quarters = [product(QUARTER * q + 256 * t) for q in range(4)]
            cols = pl.ds(256 * t, 256)
            for b in range(BLOCKS // 2):
                first, second = pack([x[8 * b : 8 * b + 8] for x in quarters])
                snd[c, 2 * b, :, cols] = first.astype(BF16)
                snd[c, 2 * b + 1, :, cols] = second.astype(BF16)
        for k in FAR_FIRST:
            to = lax.rem(z + k, 8)
            remote(
                snd.at[c, to], rsbuf.at[turn, c // 2, m], rs_s.at[0], rs_r.at[turn, c // 2],
                section=owner, mp=to + 8 * (c % 2),
            ).start()

    def share(start, size):
        rows = pl.ds(pl.multiple_of(start, CH), size)
        local(up.at[rows, feature_cols(0)], ux.at[0, rows], own_s.at[1]).start()
        for k in (2, 1, 3):
            peer = lax.rem(d + k, 4)
            remote(gx.at[0, rows], gx.at[4 - k, rows], dp_s.at[2], dp_r.at[2], dp=peer).start()
            remote(up.at[rows, feature_cols(k)], ux.at[4 - k, rows], dp_s.at[3], dp_r.at[3], dp=peer).start()

    @pl.when(s == 3)
    def _():
        tg_load.wait()

        def hidden_tile(j, carry):
            cols = pl.ds(pl.multiple_of(j * 256, 256), 256)
            cols_up = pl.ds(pl.multiple_of(UNITS + j * 256, 256), 256)
            grad_hidden = dot_nt(up[...], dw[cols, :])
            gx[0, :, cols] = (grad_hidden * slope[:, cols]).astype(BF16)
            gx[0, :, cols_up] = (grad_hidden * gated[:, cols]).astype(BF16)
            return carry

        lax.fori_loop(0, UNITS // 256, hidden_tile, 0)

        def chunk_step(c, carry):
            rows = pl.ds(pl.multiple_of(CH * c, CH), CH)
            send_partials(c, lambda at: dot_nt(gx[0, rows, :], w[pl.ds(at, 256), :]))
            return carry

        lax.fori_loop(0, CHUNKS, chunk_step, 0)
        bulk()
        share(0, ROWS)

    @pl.when(s < 3)
    def _():
        def chunk_step(c, carry):
            rows = pl.ds(pl.multiple_of(CH * c, CH), CH)
            remote(agbuf.at[c], agbuf.at[c], rs_s.at[0], ag_r.at[c], mp=m).wait_recv()
            unpack(agbuf, c, up)
            grad_hidden = dot_nn(up[rows, :], dwt[...])
            gx[0, rows, pl.ds(0, UNITS)] = (grad_hidden * slope[rows, :]).astype(BF16)
            gx[0, rows, pl.ds(UNITS, UNITS)] = (grad_hidden * gated[rows, :]).astype(BF16)
            send_partials(c, lambda at: dot_nn(gx[0, rows, :], wt[:, pl.ds(at, 256)]))

            @pl.when(s == 0)
            def _():
                share(CH * c, CH)

            @pl.when((s > 0) & (c % 4 == 3))
            def _():
                share((c // 4) * 128, 128)

            @pl.when(c % 4 == 3)
            def _():
                half = pl.ds(pl.multiple_of((c // 4) * 4, 4), 4)
                remote(agbuf.at[half], igbuf.at[half], fw_s.at[0], ig_r.at[c // 4], section=below).start()

            return carry

        lax.fori_loop(0, CHUNKS, chunk_step, 0)

    @pl.when(s == 3)
    def _():
        own_rows_ready(0)
        own_rows_ready(1)

        def from_inc(i):
            remote(incb.at[i], incb.at[i], inc_s.at[0], inc_r.at[i], mp=m).wait_recv()
            return incb[i].astype(F32)

        reduce_layer(0, from_inc, gather_to(0, agbuf, ag_r))
        reduce_layer(1, from_rout, gather_to(0, igbuf, ig_r))

    others = pl.ds(1, 3)
    for cp in late:
        cp.wait()
    own_ng.wait()
    local(ux.at[0], ux.at[0], own_s.at[1]).wait()
    remote(ngx.at[others], ngx.at[others], dp_s.at[0], dp_r.at[0], mp=m).wait_recv()
    remote(hx.at[others], hx.at[others], dp_s.at[1], dp_r.at[1], mp=m).wait_recv()
    for k in range(4):
        ngt[:, pl.ds(ROWS * k, ROWS)] = ngx[k].T
    remote(ux.at[others], ux.at[others], dp_s.at[3], dp_r.at[3], mp=m).wait_recv()
    for k in range(4):
        uxt[:, pl.ds(ROWS * k, ROWS)] = ux[k].T

    def down_tile(j, carry):
        cols = pl.ds(pl.multiple_of(j * 256, 256), 256)
        hidden = hx[:, :, cols].reshape(4 * ROWS, 256)
        down_sum = dot_nn(uxt[...], hidden)
        new_first = 0.9 * fm[:, cols] + 0.1 * down_sum
        new_second = 0.95 * sm[:, cols] + 0.05 * down_sum * down_sum
        ad[0, :, cols] = new_first / first_fix / (jnp.sqrt(new_second / second_fix) + 1e-08)
        return carry

    lax.fori_loop(0, UNITS // 256, down_tile, 0)
    remote(gx.at[others], gx.at[others], dp_s.at[2], dp_r.at[2], mp=m).wait_recv()

    def grad_tile(j, carry):
        cols = pl.ds(pl.multiple_of(j * 256, 256), 256)
        cols_up = pl.ds(pl.multiple_of(UNITS + j * 256, 256), 256)
        gate = gx[:, :, cols].reshape(4 * ROWS, 256)
        gg[0, :, cols] = dot_nn(ngt[...], gate).astype(BF16)
        upg = gx[:, :, cols_up].reshape(4 * ROWS, 256)
        ug[0, :, cols] = dot_nn(ngt[...], upg).astype(BF16)
        return carry

    lax.fori_loop(0, UNITS // 256, grad_tile, 0)

    @pl.when(s > 0)
    def _():
        for h in range(2):
            half = pl.ds(4 * h, 4)
            remote(igbuf.at[half], igbuf.at[half], rs_s.at[0], ig_r.at[h], mp=m).wait_recv()

    def last_chunk(c, carry):
        @pl.when(s == 0)
        def _():
            remote(igbuf.at[c], igbuf.at[c], rs_s.at[0], ig_r.at[c], mp=m).wait_recv()

        unpack(igbuf, c, ig.at[0])
        return carry

    lax.fori_loop(0, CHUNKS, last_chunk, 0)

    li_send.wait_send()
    gn_send.wait_send()
    remote(snd, snd, rs_s.at[0], rs_r.at[0, 0], mp=m).wait_send()
    remote(ngx.at[others], ngx.at[others], dp_s.at[0], dp_r.at[0], mp=m).wait_send()
    remote(hx.at[others], hx.at[others], dp_s.at[1], dp_r.at[1], mp=m).wait_send()
    remote(gx.at[others], gx.at[others], dp_s.at[2], dp_r.at[2], mp=m).wait_send()
    remote(ux.at[others], ux.at[others], dp_s.at[3], dp_r.at[3], mp=m).wait_send()

    @pl.when(s < 3)
    def _():
        remote(agbuf, agbuf, fw_s.at[0], ag_r.at[0], mp=m).wait_send()

    @pl.when(s == 0)
    def _():
        wait_gather_sends()
        remote(rout.at[1], incb, inc_s.at[0], inc_r.at[0], mp=m).wait_send()

    @pl.when(s == 3)
    def _():
        wait_gather_sends()


def hand_on(*refs):
    sources, targets, sems = refs[:4], refs[4:8], refs[8]
    copies = [pltpu.make_async_copy(a, b, sems.at[i]) for i, (a, b) in enumerate(zip(sources, targets))]
    for cp in copies:
        cp.start()
    for cp in copies:
        cp.wait()


def on_device(layer_input, top_grad, norm_gain, gate_weight, up_weight, down_weight, first_moment, second_moment):
    V, DMA = pltpu.VMEM, pltpu.SemaphoreType.DMA
    pieces = (16, QUARTER)
    shapes = (
        jax.ShapeDtypeStruct((1, ROWS, D), BF16),
        jax.ShapeDtypeStruct((1, 512, UNITS), BF16),
        jax.ShapeDtypeStruct((1, 512, UNITS), BF16),
        jax.ShapeDtypeStruct((1, 512, UNITS), F32),
    )
    norm_gain = pltpu.with_memory_space_constraint(norm_gain, pltpu.HBM)
    results = pl.pallas_call(
        kernel,
        out_shape=shapes,
        in_specs=[pl.BlockSpec(memory_space=pltpu.HBM)] * 8,
        out_specs=[pl.BlockSpec(memory_space=pltpu.VMEM)] * 4,
        scratch_shapes=[
            V((ROWS, D), BF16),
            V((D, 2 * UNITS), BF16),
            V((UNITS, D), BF16),
            V((2 * UNITS, D), BF16),
            V((D, UNITS), BF16),
            V((ROWS, D), BF16),
            V((1, D), F32),
            V((512, UNITS), F32),
            V((512, UNITS), F32),
            V((ROWS, D), BF16),
            V((ROWS, UNITS), F32),
            V((ROWS, UNITS), F32),
            V((4, ROWS, 2 * UNITS), BF16),
            V((4, ROWS, UNITS), BF16),
            V((4, ROWS, 512), BF16),
            V((4, ROWS, 512), BF16),
            V((512, 4 * ROWS), BF16),
            V((512, 4 * ROWS), BF16),
            V((CHUNKS, BLOCKS) + pieces, BF16),
            V((2, TURNS, 16) + pieces, BF16),
            V((2, TURNS) + pieces, BF16),
            V((CHUNKS, BLOCKS) + pieces, BF16),
            V((CHUNKS, BLOCKS) + pieces, BF16),
            V((TURNS,) + pieces, BF16),
            V((2, TURNS) + pieces, BF16),
            V((2, 1, D), F32),
            V((TURNS,) + pieces, BF16),
            V((TURNS, 16, D), BF16),
            DMA((8 + TURNS,)),
            DMA((2, TURNS)),
            DMA((CHUNKS,)),
            DMA((CHUNKS,)),
            DMA((2,)),
            DMA((2,)),
            DMA((TURNS,)),
            DMA((4,)),
            DMA((1,)),
            DMA((2,)),
            DMA((1,)),
            DMA((1,)),
            DMA((1,)),
            DMA((1,)),
            DMA((4,)),
            DMA((2,)),
        ],
        compiler_params=pltpu.CompilerParams(
            has_side_effects=True, collective_id=0, vmem_limit_bytes=50 * 1024 * 1024
        ),
        name="relay",
    )(layer_input, top_grad, norm_gain, gate_weight, up_weight, down_weight, first_moment, second_moment)
    return pl.pallas_call(
        hand_on,
        out_shape=shapes,
        in_specs=[pl.BlockSpec(memory_space=pltpu.VMEM)] * 4,
        out_specs=[pl.BlockSpec(memory_space=pltpu.HBM)] * 4,
        scratch_shapes=[DMA((4,))],
        compiler_params=pltpu.CompilerParams(vmem_limit_bytes=8 * 1024 * 1024),
        name="hand_on",
    )(*results)


def solution(mesh):
    return jax.shard_map(
        on_device,
        mesh=mesh,
        in_specs=(
            P("section", "dp", None),
            P("dp", None),
            P("section", None),
            P("section", None, "mp"),
            P("section", None, "mp"),
            P("section", "mp", None),
            P("section", "dp", "mp"),
            P("section", "dp", "mp"),
        ),
        out_specs=(
            P("section", "dp", None),
            P("section", "dp", "mp"),
            P("section", "dp", "mp"),
            P("section", "dp", "mp"),
        ),
        check_vma=False,
    )
```

time: 112 us -> 89 us (0.79)
  Pallas kernels: 107 us -> 87.6 us
  local copies, waits for them, and re-layouts: 4.22 us -> 0 us
    pallas_call x1 -> x2, Pallas kernels: 107 us -> 87.6 us  [the longest x1 85.9 us: on_device(): pl.pallas_call(kernel, out_shape=shapes, in_specs=[pl.BlockSpec(memory_sp...]
    unnamed x6 -> x0, local copies, waits for them, and re-layouts: 4.22 us -> none
where the time goes in v2:
time: 89 us; the launch traced here: 88.3 us
  Pallas kernels  87.6 us (98%)
    pallas_call x1, Pallas kernels, on_device(): pl.pallas_call(kernel, out_shape=shapes, in_specs=[pl.BlockSpec(memory_sp...  85.9 us

profile of v2, /device:TPU:2, one launch (start us, length us, event | category | flops | bytes accessed | tf_op | source)
XLA Modules:
  0.0 88.3 jit_solution(16277064993175526438)
XLA Ops:
  0.6 85.9 %relay.1 = (bf16[1,256,2048]{2,1,0:T(8,128)(2,1)S(1)}, bf16[1,512,512]{2,1,0:T(8,128)(2,1)S(1)}, bf16[1,512,512]{2,1,0:T(8,128)(2,1)S(1)}, f32[1,512,512]{2,1,0:T(8,128)S(1)}) custom-call(bf16[1,256,2048]{2,1,0:T(8,128)(2,1)} %li_h.1, bf16[256,2048]{1,0:T(8,128)(2,1)} %tg_h.1, f32[1,2048]{1,0:T(1,128)} %gain_h.1, bf16[1,2048,512]{2,1,0:T(8,128)(2,1)} %gw_h.1, ...), custom_call_target="tpu_custom_call" | custom-call | tf_op jit(solution)/shard_map/relay/pallas_call | solution.py:487
  86.6 1.7 %hand_on.1 = (bf16[1,256,2048]{2,1,0:T(8,128)(2,1)}, bf16[1,512,512]{2,1,0:T(8,128)(2,1)}, bf16[1,512,512]{2,1,0:T(8,128)(2,1)}, f32[1,512,512]{2,1,0:T(8,128)}) custom-call(bf16[1,256,2048]{2,1,0:T(8,128)(2,1)S(1)} %get-tuple-element.8.refs_0_, bf16[1,512,512]{2,1,0:T(8,128)(2,1)S(1)} %get-tuple-element.9.refs_1_, ...), custom_call_target="tpu_custom_call" | custom-call | tf_op jit(solution)/shard_map/hand_on/pallas_call | solution.py:543

commit v3 on v2

--- a/solution.py
+++ b/solution.py
@@ -20,6 +20,7 @@
 CH = ROWS // CHUNKS
 BLOCKS = CH // 4
 TURNS = CHUNKS // 2
+EARLY = 4
 FAR_FIRST = (4, 3, 5, 2, 6, 1, 7, 0)
 
 
@@ -65,10 +66,10 @@
     li_h, tg_h, gain_h, gw_h, uw_h, dw_h, fm_h, sm_h,
     ig, gg, ug, ad,
     li, w, dw, wt, dwt, up, gain, fm, sm,
-    ng, gated, slope, gx, hx, ngx, ux, ngt, uxt,
-    snd, rsbuf, rout, agbuf, igbuf,
-    lisend, liown, gnown, incb, tgown,
-    ld, rs_r, ag_r, ig_r, li_r, gn_r, inc_r, dp_r,
+    ng, gated, slope, gh, gx, hx, ngx, ux, ngt, uxt, acc,
+    snd, rsbuf, rs2, rout, rout2, agbuf, igbuf,
+    lisend, liown, liown2, gnown, gnown2, incb, inc2, tgown,
+    ld, rs_r, rs2_r, ag_r, ig_r, li_r, gn_r, inc_r, inc2_r, dp_r,
     rs_s, ag_s, inc_s, li_s, gn_s, fw_s, dp_s, own_s,
 ):
     d = lax.axis_index("dp")
@@ -97,25 +98,6 @@
 
     tg_rows = [local(tg_h.at[own_tile(i)], tgown.at[i], ld.at[8 + i]) for i in range(TURNS)]
 
-    li_load.start()
-    gain_load.start()
-
-    @pl.when(s == 3)
-    def _():
-        tg_load.start()
-
-    gw_load.start()
-    uw_load.start()
-    dw_load.start()
-
-    @pl.when(s == 0)
-    def _():
-        for cp in tg_rows:
-            cp.start()
-
-    for cp in late:
-        cp.start()
-
     barrier = pltpu.get_barrier_semaphore()
 
     def greet(**to):
@@ -127,28 +109,50 @@
             return carry
         lax.fori_loop(0, 16, one, 0)
 
+    @pl.when(s == 3)
+    def _():
+        greet_all(0)
+        greet_all(1)
+        greet_all(2)
+
+    @pl.when(s == 2)
+    def _():
+        greet_all(0)
+        greet(section=1)
+
+    @pl.when(s == 1)
+    def _():
+        greet_all(0)
+        greet_all(3)
+
+    @pl.when(s == 0)
+    def _():
+        greet_all(3)
+        greet_all(2)
+
     for k in (1, 2, 3):
         greet(dp=lax.rem(d + k, 4))
 
+    li_load.start()
+    gain_load.start()
+
     @pl.when(s == 3)
     def _():
-        greet_all(0)
-        greet_all(1)
-        greet(section=2)
-
-    @pl.when(s == 2)
-    def _():
-        greet_all(0)
-        greet(section=1)
-
-    @pl.when(s == 1)
-    def _():
-        greet_all(0)
+        tg_load.start()
+
+    dw_load.start()
+    gw_load.start()
+    uw_load.start()
 
     @pl.when(s == 0)
     def _():
-        greet_all(3)
-        greet_all(2)
+        for cp in tg_rows:
+            cp.start()
+
+    for cp in late:
+        cp.start()
+
+    early, later = pl.ds(0, 2), pl.ds(2, 2)
 
     def own_piece(tile):
         tile = tile.astype(F32)
@@ -158,8 +162,6 @@
 
     li_load.wait()
     gain_load.wait()
-    for i in range(TURNS):
-        lisend[i] = own_piece(li[own_tile(i), :]).astype(BF16)
     li_send = remote(lisend, liown.at[turn], li_s.at[0], li_r.at[turn], section=owner)
     gn_send = remote(gain, gnown.at[turn], gn_s.at[0], gn_r.at[turn], section=owner)
 
@@ -171,6 +173,22 @@
         return carry
 
     lax.fori_loop(0, ROWS // 32, norm_rows, 0)
+    dw_load.wait()
+
+    @pl.when(s == 3)
+    def _():
+        tg_load.wait()
+
+        def hidden_tile(j, carry):
+            cols = pl.ds(pl.multiple_of(j * 256, 256), 256)
+            gh[:, cols] = dot_nt(up[...], dw[cols, :])
+            return carry
+
+        lax.fori_loop(0, UNITS // 256, hidden_tile, 0)
+
+    for i in range(TURNS):
+        lisend[i] = own_piece(li[own_tile(i), :]).astype(BF16)
+
     gw_load.wait()
     uw_load.wait()
 
@@ -188,11 +206,11 @@
 
     lax.fori_loop(0, UNITS // 256, forward, 0)
 
-    @pl.when(s == 3)
-    def _():
-        pl.semaphore_wait(barrier, 19)
-
-    @pl.when((s == 2) | (s == 1))
+    @pl.when(s >= 2)
+    def _():
+        pl.semaphore_wait(barrier, 35)
+
+    @pl.when(s == 1)
     def _():
         pl.semaphore_wait(barrier, 20)
 
@@ -202,7 +220,13 @@
 
     li_send.start()
     gn_send.start()
-    dw_load.wait()
+    li_later = remote(lisend.at[later], liown2, li_s.at[1], li_r.at[2], section=3)
+    gn_later = remote(gain, gnown2, gn_s.at[1], gn_r.at[2], section=3)
+
+    @pl.when(s == 2)
+    def _():
+        li_later.start()
+        gn_later.start()
 
     def feature_cols(k):
         return pl.ds(pl.multiple_of(lax.rem(d + k, 4) * 512, 512), 512)
@@ -216,36 +240,39 @@
             remote(ng.at[:, feature_cols(k)], ngx.at[4 - k], dp_s.at[0], dp_r.at[0], dp=peer).start()
             remote(hx.at[0], hx.at[4 - k], dp_s.at[1], dp_r.at[1], dp=peer).start()
 
-    def reduce_layer(u, incoming, sends):
+    def reduce_layer(buf, sem, own_rows, own_gain, out, incoming, sends, first, stop):
         def chunk(i, carry):
-            remote(rsbuf.at[u, i], rsbuf.at[u, i], rs_s.at[0], rs_r.at[u, i], mp=m).wait_recv()
-            values = liown[u, i].astype(F32)
+            remote(buf.at[i], buf.at[i], rs_s.at[0], sem.at[i], mp=m).wait_recv()
+            values = own_rows[i].astype(F32)
             scale_inv = lax.rsqrt(row_sums(values * values) * (1.0 / D) + 1e-05)
             normed = values * scale_inv
-            total = rsbuf[u, i, 0].astype(F32)
+            total = buf[i, 0].astype(F32)
             for k in range(1, 16):
-                total = total + rsbuf[u, i, k].astype(F32)
+                total = total + buf[i, k].astype(F32)
             quarter = lax.broadcasted_iota(jnp.int32, (16, QUARTER), 0) // 4
             gain_piece = jnp.zeros((16, QUARTER), F32)
             for q in range(4):
-                gain_piece = jnp.where(quarter == q, gnown[u, :, pl.ds(QUARTER * q, QUARTER)], gain_piece)
+                gain_piece = jnp.where(quarter == q, own_gain[:, pl.ds(QUARTER * q, QUARTER)], gain_piece)
             scaled = total * gain_piece
             projection = row_sums(scaled * normed) * (1.0 / D)
-            rout[u, i] = (incoming(i) + scale_inv * (scaled - normed * projection)).astype(BF16)
-            sends(u, i)
-            return carry
-
-        lax.fori_loop(0, TURNS, chunk, 0)
-
-    def gather_to(section, buf, sem):
-        def sends(u, i):
-            chunk = yh + 2 * i
+            out[i] = (incoming(i) + scale_inv * (scaled - normed * projection)).astype(BF16)
+            sends(i)
+            return carry
+
+        lax.fori_loop(first, stop, chunk, 0)
+
+    def reduce_turn(u, incoming, sends, first, stop):
+        reduce_layer(
+            rsbuf.at[u], rs_r.at[u], liown.at[u], gnown.at[u], rout.at[u], incoming, sends, first, stop
+        )
+
+    def gather_to(section, buf, sem, out, ssem, base=0):
+        def sends(i):
+            chunk = yh + 2 * (i + base)
             for k in FAR_FIRST:
                 for h in range(2):
                     to = lax.rem(z + k, 8) + 8 * h
-                    remote(
-                        rout.at[u, i], buf.at[chunk, z], ag_s.at[u], sem.at[chunk], section=section, mp=to
-                    ).start()
+                    remote(out.at[i], buf.at[chunk, z], ssem, sem.at[chunk], section=section, mp=to).start()
         return sends
 
     def own_rows_ready(u):
@@ -255,9 +282,14 @@
     def from_rout(i):
         return rout[0, i].astype(F32)
 
-    def wait_gather_sends():
-        for u in range(2):
-            remote(rsbuf.at[u], rsbuf.at[u], ag_s.at[u], rs_r.at[u, 0], mp=m).wait_send()
+    others = pl.ds(1, 3)
+
+    def turn_ng():
+        own_ng.wait()
+        remote(ngx.at[others], ngx.at[others], dp_s.at[0], dp_r.at[0], mp=m).wait_recv()
+        for h in range(2):
+            for k in range(4):
+                ngt[h, :, pl.ds(128 * k, 128)] = ngx[k, pl.ds(128 * h, 128), :].T
 
     @pl.when(s < 3)
     def _():
@@ -287,12 +319,23 @@
         def from_top(i):
             return own_piece(tgown[i])
 
-        def sends_two(u, i):
-            gather_to(1, agbuf, ag_r)(u, i)
-            remote(rout.at[u, i], incb.at[i], inc_s.at[0], inc_r.at[i], section=3).start()
-
-        reduce_layer(0, from_top, gather_to(2, agbuf, ag_r))
-        reduce_layer(1, from_rout, sends_two)
+        to_two = gather_to(2, agbuf, ag_r, rout.at[0], ag_s.at[0])
+        to_one = gather_to(1, agbuf, ag_r, rout.at[1], ag_s.at[1])
+
+        def sends_three(i):
+            to_two(i)
+
+            @pl.when(i >= 2)
+            def _():
+                remote(rout.at[0, i], inc2.at[i % 2], inc_s.at[1], inc2_r.at[i % 2], section=3).start()
+
+        def sends_two(i):
+            to_one(i)
+            remote(rout.at[1, i], incb.at[i], inc_s.at[0], inc_r.at[i], section=3).start()
+
+        reduce_turn(0, from_top, sends_three, 0, TURNS)
+        reduce_turn(1, from_rout, sends_two, 0, 2)
+        turn_ng()
 
     below = jnp.where(s == 3, 0, s + 1)
 
@@ -313,34 +356,40 @@
                 first, second = pack([x[8 * b : 8 * b + 8] for x in quarters])
                 snd[c, 2 * b, :, cols] = first.astype(BF16)
                 snd[c, 2 * b + 1, :, cols] = second.astype(BF16)
-        for k in FAR_FIRST:
-            to = lax.rem(z + k, 8)
-            remote(
-                snd.at[c, to], rsbuf.at[turn, c // 2, m], rs_s.at[0], rs_r.at[turn, c // 2],
-                section=owner, mp=to + 8 * (c % 2),
-            ).start()
+
+        moved = (s == 2) & (c >= 4)
+
+        @pl.when(moved)
+        def _():
+            for k in FAR_FIRST:
+                to = lax.rem(z + k, 8)
+                remote(
+                    snd.at[c, to], rs2.at[(c // 2) % 2, m], rs_s.at[0], rs2_r.at[(c // 2) % 2],
+                    section=3, mp=to + 8 * (c % 2),
+                ).start()
+
+        @pl.when(jnp.logical_not(moved))
+        def _():
+            for k in FAR_FIRST:
+                to = lax.rem(z + k, 8)
+                remote(
+                    snd.at[c, to], rsbuf.at[turn, c // 2, m], rs_s.at[0], rs_r.at[turn, c // 2],
+                    section=owner, mp=to + 8 * (c % 2),
+                ).start()
 
     def share(start, size):
         rows = pl.ds(pl.multiple_of(start, CH), size)
-        local(up.at[rows, feature_cols(0)], ux.at[0, rows], own_s.at[1]).start()
+        half = start // 128
+        local(up.at[rows, feature_cols(0)], ux.at[0, rows], own_s.at[1 + half]).start()
         for k in (2, 1, 3):
             peer = lax.rem(d + k, 4)
-            remote(gx.at[0, rows], gx.at[4 - k, rows], dp_s.at[2], dp_r.at[2], dp=peer).start()
-            remote(up.at[rows, feature_cols(k)], ux.at[4 - k, rows], dp_s.at[3], dp_r.at[3], dp=peer).start()
+            remote(gx.at[0, rows], gx.at[4 - k, rows], dp_s.at[2], dp_r.at[2 + half], dp=peer).start()
+            remote(up.at[rows, feature_cols(k)], ux.at[4 - k, rows], dp_s.at[3], dp_r.at[4 + half], dp=peer).start()
 
     @pl.when(s == 3)
     def _():
-        tg_load.wait()
-
-        def hidden_tile(j, carry):
-            cols = pl.ds(pl.multiple_of(j * 256, 256), 256)
-            cols_up = pl.ds(pl.multiple_of(UNITS + j * 256, 256), 256)
-            grad_hidden = dot_nt(up[...], dw[cols, :])
-            gx[0, :, cols] = (grad_hidden * slope[:, cols]).astype(BF16)
-            gx[0, :, cols_up] = (grad_hidden * gated[:, cols]).astype(BF16)
-            return carry
-
-        lax.fori_loop(0, UNITS // 256, hidden_tile, 0)
+        gx[0, :, pl.ds(0, UNITS)] = (gh[...] * slope[...]).astype(BF16)
+        gx[0, :, pl.ds(UNITS, UNITS)] = (gh[...] * gated[...]).astype(BF16)
 
         def chunk_step(c, carry):
             rows = pl.ds(pl.multiple_of(CH * c, CH), CH)
@@ -349,7 +398,8 @@
 
         lax.fori_loop(0, CHUNKS, chunk_step, 0)
         bulk()
-        share(0, ROWS)
+        share(0, 128)
+        share(128, 128)
 
     @pl.when(s < 3)
     def _():
@@ -383,55 +433,35 @@
     def _():
         own_rows_ready(0)
         own_rows_ready(1)
+        remote(liown2, liown2, li_s.at[0], li_r.at[2], mp=m).wait_recv()
+        remote(gnown2, gnown2, gn_s.at[0], gn_r.at[2], mp=m).wait_recv()
+
+        def from_above(i):
+            remote(inc2.at[i], inc2.at[i], inc_s.at[0], inc2_r.at[i], mp=m).wait_recv()
+            return inc2[i].astype(F32)
 
         def from_inc(i):
             remote(incb.at[i], incb.at[i], inc_s.at[0], inc_r.at[i], mp=m).wait_recv()
             return incb[i].astype(F32)
 
-        reduce_layer(0, from_inc, gather_to(0, agbuf, ag_r))
-        reduce_layer(1, from_rout, gather_to(0, igbuf, ig_r))
-
-    others = pl.ds(1, 3)
+        def from_later(i):
+            return rout2[i % 2].astype(F32)
+
+        to_one = gather_to(1, agbuf, ag_r, rout2, ag_s.at[2], 2)
+        reduce_layer(rs2, rs2_r, liown2, gnown2, rout2, from_above, to_one, 0, 2)
+        to_zero = gather_to(0, agbuf, ag_r, rout.at[0], ag_s.at[0])
+        reduce_turn(0, from_inc, to_zero, 0, 2)
+        reduce_turn(0, from_later, to_zero, 2, TURNS)
+        reduce_turn(1, from_rout, gather_to(0, igbuf, ig_r, rout.at[1], ag_s.at[1]), 0, TURNS)
+
     for cp in late:
         cp.wait()
-    own_ng.wait()
-    local(ux.at[0], ux.at[0], own_s.at[1]).wait()
-    remote(ngx.at[others], ngx.at[others], dp_s.at[0], dp_r.at[0], mp=m).wait_recv()
+
+    @pl.when(s > 0)
+    def _():
+        turn_ng()
+
     remote(hx.at[others], hx.at[others], dp_s.at[1], dp_r.at[1], mp=m).wait_recv()
-    for k in range(4):
-        ngt[:, pl.ds(ROWS * k, ROWS)] = ngx[k].T
-    remote(ux.at[others], ux.at[others], dp_s.at[3], dp_r.at[3], mp=m).wait_recv()
-    for k in range(4):
-        uxt[:, pl.ds(ROWS * k, ROWS)] = ux[k].T
-
-    def down_tile(j, carry):
-        cols = pl.ds(pl.multiple_of(j * 256, 256), 256)
-        hidden = hx[:, :, cols].reshape(4 * ROWS, 256)
-        down_sum = dot_nn(uxt[...], hidden)
-        new_first = 0.9 * fm[:, cols] + 0.1 * down_sum
-        new_second = 0.95 * sm[:, cols] + 0.05 * down_sum * down_sum
-        ad[0, :, cols] = new_first / first_fix / (jnp.sqrt(new_second / second_fix) + 1e-08)
-        return carry
-
-    lax.fori_loop(0, UNITS // 256, down_tile, 0)
-    remote(gx.at[others], gx.at[others], dp_s.at[2], dp_r.at[2], mp=m).wait_recv()
-
-    def grad_tile(j, carry):
-        cols = pl.ds(pl.multiple_of(j * 256, 256), 256)
-        cols_up = pl.ds(pl.multiple_of(UNITS + j * 256, 256), 256)
-        gate = gx[:, :, cols].reshape(4 * ROWS, 256)
-        gg[0, :, cols] = dot_nn(ngt[...], gate).astype(BF16)
-        upg = gx[:, :, cols_up].reshape(4 * ROWS, 256)
-        ug[0, :, cols] = dot_nn(ngt[...], upg).astype(BF16)
-        return carry
-
-    lax.fori_loop(0, UNITS // 256, grad_tile, 0)
-
-    @pl.when(s > 0)
-    def _():
-        for h in range(2):
-            half = pl.ds(4 * h, 4)
-            remote(igbuf.at[half], igbuf.at[half], rs_s.at[0], ig_r.at[h], mp=m).wait_recv()
 
     def last_chunk(c, carry):
         @pl.when(s == 0)
@@ -441,7 +471,51 @@
         unpack(igbuf, c, ig.at[0])
         return carry
 
-    lax.fori_loop(0, CHUNKS, last_chunk, 0)
+    for h in range(2):
+        rows = pl.ds(128 * h, 128)
+        local(ux.at[0, rows], ux.at[0, rows], own_s.at[1 + h]).wait()
+        remote(ux.at[others, rows], ux.at[others, rows], dp_s.at[3], dp_r.at[4 + h], mp=m).wait_recv()
+        for k in range(4):
+            uxt[h, :, pl.ds(128 * k, 128)] = ux[k, rows, :].T
+        remote(gx.at[others, rows], gx.at[others, rows], dp_s.at[2], dp_r.at[2 + h], mp=m).wait_recv()
+
+        def grad_tile(j, carry):
+            cols = pl.ds(pl.multiple_of(j * 256, 256), 256)
+            cols_up = pl.ds(pl.multiple_of(UNITS + j * 256, 256), 256)
+            down_sum = dot_nn(uxt[h], hx[:, rows, cols].reshape(2 * ROWS, 256))
+            gate_sum = dot_nn(ngt[h], gx[:, rows, cols].reshape(2 * ROWS, 256))
+            up_sum = dot_nn(ngt[h], gx[:, rows, cols_up].reshape(2 * ROWS, 256))
+            if h == 0:
+                acc[0, :, cols] = down_sum
+                acc[1, :, cols] = gate_sum
+                acc[2, :, cols] = up_sum
+            else:
+                down_sum = down_sum + acc[0, :, cols]
+                gg[0, :, cols] = (gate_sum + acc[1, :, cols]).astype(BF16)
+                ug[0, :, cols] = (up_sum + acc[2, :, cols]).astype(BF16)
+                new_first = 0.9 * fm[:, cols] + 0.1 * down_sum
+                new_second = 0.95 * sm[:, cols] + 0.05 * down_sum * down_sum
+                ad[0, :, cols] = new_first / first_fix / (jnp.sqrt(new_second / second_fix) + 1e-08)
+            return carry
+
+        lax.fori_loop(0, UNITS // 256, grad_tile, 0)
+
+        if h == 0:
+            @pl.when(s == 0)
+            def _():
+                lax.fori_loop(0, EARLY, last_chunk, 0)
+
+    @pl.when(s > 0)
+    def _():
+        for h in range(2):
+            half = pl.ds(4 * h, 4)
+            remote(igbuf.at[half], igbuf.at[half], rs_s.at[0], ig_r.at[h], mp=m).wait_recv()
+
+    @pl.when(s > 0)
+    def _():
+        lax.fori_loop(0, EARLY, last_chunk, 0)
+
+    lax.fori_loop(EARLY, CHUNKS, last_chunk, 0)
 
     li_send.wait_send()
     gn_send.wait_send()
@@ -455,14 +529,23 @@
     def _():
         remote(agbuf, agbuf, fw_s.at[0], ag_r.at[0], mp=m).wait_send()
 
+    @pl.when(s == 2)
+    def _():
+        li_later.wait_send()
+        gn_later.wait_send()
+
     @pl.when(s == 0)
     def _():
-        wait_gather_sends()
-        remote(rout.at[1], incb, inc_s.at[0], inc_r.at[0], mp=m).wait_send()
+        remote(rsbuf.at[0], rsbuf.at[0], ag_s.at[0], rs_r.at[0, 0], mp=m).wait_send()
+        remote(rsbuf.at[1, early], rsbuf.at[1, early], ag_s.at[1], rs_r.at[0, 0], mp=m).wait_send()
+        remote(rout.at[1, early], incb, inc_s.at[0], inc_r.at[0], mp=m).wait_send()
+        remote(rout.at[0, later], inc2, inc_s.at[1], inc_r.at[0], mp=m).wait_send()
 
     @pl.when(s == 3)
     def _():
-        wait_gather_sends()
+        for u in range(2):
+            remote(rsbuf.at[u], rsbuf.at[u], ag_s.at[u], rs_r.at[0, 0], mp=m).wait_send()
+        remote(rs2, rs2, ag_s.at[2], rs_r.at[0, 0], mp=m).wait_send()
 
 
 def hand_on(*refs):
@@ -502,38 +585,47 @@
             V((ROWS, D), BF16),
             V((ROWS, UNITS), F32),
             V((ROWS, UNITS), F32),
+            V((ROWS, UNITS), F32),
             V((4, ROWS, 2 * UNITS), BF16),
             V((4, ROWS, UNITS), BF16),
             V((4, ROWS, 512), BF16),
             V((4, ROWS, 512), BF16),
-            V((512, 4 * ROWS), BF16),
-            V((512, 4 * ROWS), BF16),
+            V((2, 512, 2 * ROWS), BF16),
+            V((2, 512, 2 * ROWS), BF16),
+            V((3, 512, UNITS), F32),
             V((CHUNKS, BLOCKS) + pieces, BF16),
             V((2, TURNS, 16) + pieces, BF16),
+            V((2, 16) + pieces, BF16),
             V((2, TURNS) + pieces, BF16),
+            V((2,) + pieces, BF16),
             V((CHUNKS, BLOCKS) + pieces, BF16),
             V((CHUNKS, BLOCKS) + pieces, BF16),
             V((TURNS,) + pieces, BF16),
             V((2, TURNS) + pieces, BF16),
+            V((2,) + pieces, BF16),
             V((2, 1, D), F32),
-            V((TURNS,) + pieces, BF16),
+            V((1, D), F32),
+            V((2,) + pieces, BF16),
+            V((2,) + pieces, BF16),
             V((TURNS, 16, D), BF16),
             DMA((8 + TURNS,)),
             DMA((2, TURNS)),
+            DMA((2,)),
             DMA((CHUNKS,)),
             DMA((CHUNKS,)),
+            DMA((3,)),
+            DMA((3,)),
             DMA((2,)),
             DMA((2,)),
-            DMA((TURNS,)),
-            DMA((4,)),
+            DMA((6,)),
             DMA((1,)),
+            DMA((3,)),
+            DMA((2,)),
+            DMA((2,)),
             DMA((2,)),
             DMA((1,)),
-            DMA((1,)),
-            DMA((1,)),
-            DMA((1,)),
             DMA((4,)),
-            DMA((2,)),
+            DMA((3,)),
         ],
         compiler_params=pltpu.CompilerParams(
             has_side_effects=True, collective_id=0, vmem_limit_bytes=50 * 1024 * 1024

time: 89 us -> 86.9 us (0.976)
  Pallas kernels: 87.6 us -> 86.2 us
    pallas_call x1, Pallas kernels: 85.9 us -> 84.5 us  [on_device(): pl.pallas_call(kernel, out_shape=shapes, in_specs=[pl.BlockSpec(memory_sp...]
where the time goes in v3:
time: 86.9 us
  Pallas kernels  86.2 us (99%)
    pallas_call x1, Pallas kernels, on_device(): pl.pallas_call(kernel, out_shape=shapes, in_specs=[pl.BlockSpec(memory_sp...  84.5 us

profile of v3, /device:TPU:2, one launch (start us, length us, event | category | flops | bytes accessed | tf_op | source)
XLA Modules:
  0.0 86.9 jit_solution(12527172994481356364)
XLA Ops:
  0.6 84.5 %relay.1 = (bf16[1,256,2048]{2,1,0:T(8,128)(2,1)S(1)}, bf16[1,512,512]{2,1,0:T(8,128)(2,1)S(1)}, bf16[1,512,512]{2,1,0:T(8,128)(2,1)S(1)}, f32[1,512,512]{2,1,0:T(8,128)S(1)}) custom-call(bf16[1,256,2048]{2,1,0:T(8,128)(2,1)} %li_h.1, bf16[256,2048]{1,0:T(8,128)(2,1)} %tg_h.1, f32[1,2048]{1,0:T(1,128)} %gain_h.1, bf16[1,2048,512]{2,1,0:T(8,128)(2,1)} %gw_h.1, ...), custom_call_target="tpu_custom_call" | custom-call | tf_op jit(solution)/shard_map/relay/pallas_call | solution.py:570
  85.2 1.7 %hand_on.1 = (bf16[1,256,2048]{2,1,0:T(8,128)(2,1)}, bf16[1,512,512]{2,1,0:T(8,128)(2,1)}, bf16[1,512,512]{2,1,0:T(8,128)(2,1)}, f32[1,512,512]{2,1,0:T(8,128)}) custom-call(bf16[1,256,2048]{2,1,0:T(8,128)(2,1)S(1)} %get-tuple-element.8.refs_0_, bf16[1,512,512]{2,1,0:T(8,128)(2,1)S(1)} %get-tuple-element.9.refs_1_, ...), custom_call_target="tpu_custom_call" | custom-call | tf_op jit(solution)/shard_map/hand_on/pallas_call | solution.py:635

commit v4 on v3

--- a/solution.py
+++ b/solution.py
@@ -22,6 +22,7 @@
 TURNS = CHUNKS // 2
 EARLY = 4
 FAR_FIRST = (4, 3, 5, 2, 6, 1, 7, 0)
+OUTER_LAST = (0, 1, 2, 7, 3, 6, 5, 4)
 
 
 def dot_nn(left, right):
@@ -87,8 +88,12 @@
 
     li_load = local(li_h.at[0], li, ld.at[0])
     gain_load = local(gain_h, gain, ld.at[1])
-    gw_load = local(gw_h.at[0], w.at[:, pl.ds(0, UNITS)], ld.at[2])
-    uw_load = local(uw_h.at[0], w.at[:, pl.ds(UNITS, UNITS)], ld.at[3])
+    w_loads = []
+    for j in range(2):
+        cols, cols_up = pl.ds(256 * j, 256), pl.ds(UNITS + 256 * j, 256)
+        gw_load = local(gw_h.at[0, :, cols], w.at[:, cols], ld.at[8 + TURNS + 2 * j])
+        uw_load = local(uw_h.at[0, :, cols], w.at[:, cols_up], ld.at[9 + TURNS + 2 * j])
+        w_loads.append((gw_load, uw_load))
     dw_load = local(dw_h.at[0], dw, ld.at[4])
     late = [local(fm_h.at[0], fm, ld.at[5]), local(sm_h.at[0], sm, ld.at[6])]
     tg_load = local(tg_h, up, ld.at[7])
@@ -141,8 +146,9 @@
         tg_load.start()
 
     dw_load.start()
-    gw_load.start()
-    uw_load.start()
+    for gw_load, uw_load in w_loads:
+        gw_load.start()
+        uw_load.start()
 
     @pl.when(s == 0)
     def _():
@@ -189,12 +195,10 @@
     for i in range(TURNS):
         lisend[i] = own_piece(li[own_tile(i), :]).astype(BF16)
 
-    gw_load.wait()
-    uw_load.wait()
-
-    def forward(j, carry):
-        cols = pl.ds(pl.multiple_of(j * 256, 256), 256)
-        cols_up = pl.ds(pl.multiple_of(UNITS + j * 256, 256), 256)
+    for j, (gw_load, uw_load) in enumerate(w_loads):
+        gw_load.wait()
+        uw_load.wait()
+        cols, cols_up = pl.ds(256 * j, 256), pl.ds(UNITS + 256 * j, 256)
         gate_pre = dot_nn(ng[...], w[:, cols])
         up_pre = dot_nn(ng[...], w[:, cols_up])
         sig = jax.nn.sigmoid(gate_pre)
@@ -202,9 +206,6 @@
         gated[:, cols] = gate
         hx[0, :, cols] = (gate * up_pre).astype(BF16)
         slope[:, cols] = up_pre * sig * (1.0 + gate_pre * (1.0 - sig))
-        return carry
-
-    lax.fori_loop(0, UNITS // 256, forward, 0)
 
     @pl.when(s >= 2)
     def _():
@@ -266,12 +267,12 @@
             rsbuf.at[u], rs_r.at[u], liown.at[u], gnown.at[u], rout.at[u], incoming, sends, first, stop
         )
 
-    def gather_to(section, buf, sem, out, ssem, base=0):
+    def gather_to(section, buf, sem, out, ssem, base=0, last=False):
         def sends(i):
             chunk = yh + 2 * (i + base)
             for k in FAR_FIRST:
                 for h in range(2):
-                    to = lax.rem(z + k, 8) + 8 * h
+                    to = (OUTER_LAST[FAR_FIRST.index(k)] if last else lax.rem(z + k, 8)) + 8 * h
                     remote(out.at[i], buf.at[chunk, z], ssem, sem.at[chunk], section=section, mp=to).start()
         return sends
 
@@ -452,7 +453,7 @@
         to_zero = gather_to(0, agbuf, ag_r, rout.at[0], ag_s.at[0])
         reduce_turn(0, from_inc, to_zero, 0, 2)
         reduce_turn(0, from_later, to_zero, 2, TURNS)
-        reduce_turn(1, from_rout, gather_to(0, igbuf, ig_r, rout.at[1], ag_s.at[1]), 0, TURNS)
+        reduce_turn(1, from_rout, gather_to(0, igbuf, ig_r, rout.at[1], ag_s.at[1], last=True), 0, TURNS)
 
     for cp in late:
         cp.wait()
@@ -608,7 +609,7 @@
             V((2,) + pieces, BF16),
             V((2,) + pieces, BF16),
             V((TURNS, 16, D), BF16),
-            DMA((8 + TURNS,)),
+            DMA((12 + TURNS,)),
             DMA((2, TURNS)),
             DMA((2,)),
             DMA((CHUNKS,)),

time: 86.9 us -> 86.7 us (level)
  no operation moved by 1% of the time
where the time goes in v4:
time: 86.7 us; the launch traced here: 86.4 us
  Pallas kernels  85.8 us (99%)
    pallas_call x1, Pallas kernels, on_device(): pl.pallas_call(kernel, out_shape=shapes, in_specs=[pl.BlockSpec(memory_sp...  84.1 us

profile of v4, /device:TPU:2, one launch (start us, length us, event | category | flops | bytes accessed | tf_op | source)
XLA Modules:
  0.0 86.4 jit_solution(14714316123693841847)
XLA Ops:
  0.6 84.1 %relay.1 = (bf16[1,256,2048]{2,1,0:T(8,128)(2,1)S(1)}, bf16[1,512,512]{2,1,0:T(8,128)(2,1)S(1)}, bf16[1,512,512]{2,1,0:T(8,128)(2,1)S(1)}, f32[1,512,512]{2,1,0:T(8,128)S(1)}) custom-call(bf16[1,256,2048]{2,1,0:T(8,128)(2,1)} %li_h.1, bf16[256,2048]{1,0:T(8,128)(2,1)} %tg_h.1, f32[1,2048]{1,0:T(1,128)} %gain_h.1, bf16[1,2048,512]{2,1,0:T(8,128)(2,1)} %gw_h.1, ...), custom_call_target="tpu_custom_call" | custom-call | tf_op jit(solution)/shard_map/relay/pallas_call | solution.py:571
  84.7 1.7 %hand_on.1 = (bf16[1,256,2048]{2,1,0:T(8,128)(2,1)}, bf16[1,512,512]{2,1,0:T(8,128)(2,1)}, bf16[1,512,512]{2,1,0:T(8,128)(2,1)}, f32[1,512,512]{2,1,0:T(8,128)}) custom-call(bf16[1,256,2048]{2,1,0:T(8,128)(2,1)S(1)} %get-tuple-element.8.refs_0_, bf16[1,512,512]{2,1,0:T(8,128)(2,1)S(1)} %get-tuple-element.9.refs_1_, ...), custom_call_target="tpu_custom_call" | custom-call | tf_op jit(solution)/shard_map/hand_on/pallas_call | solution.py:636

commit v5 on v4

--- a/solution.py
+++ b/solution.py
@@ -289,8 +289,8 @@
         own_ng.wait()
         remote(ngx.at[others], ngx.at[others], dp_s.at[0], dp_r.at[0], mp=m).wait_recv()
         for h in range(2):
-            for k in range(4):
-                ngt[h, :, pl.ds(128 * k, 128)] = ngx[k, pl.ds(128 * h, 128), :].T
+            size = (192, 64)[h]
+            ngt[:, pl.ds(768 * h, 4 * size)] = ngx[:, pl.ds(192 * h, size), :].reshape(4 * size, 512).T
 
     @pl.when(s < 3)
     def _():
@@ -380,7 +380,7 @@
 
     def share(start, size):
         rows = pl.ds(pl.multiple_of(start, CH), size)
-        half = start // 128
+        half = start // 192
         local(up.at[rows, feature_cols(0)], ux.at[0, rows], own_s.at[1 + half]).start()
         for k in (2, 1, 3):
             peer = lax.rem(d + k, 4)
@@ -399,8 +399,8 @@
 
         lax.fori_loop(0, CHUNKS, chunk_step, 0)
         bulk()
-        share(0, 128)
-        share(128, 128)
+        share(0, 192)
+        share(192, 64)
 
     @pl.when(s < 3)
     def _():
@@ -419,7 +419,8 @@
 
             @pl.when((s > 0) & (c % 4 == 3))
             def _():
-                share((c // 4) * 128, 128)
+                share((c // 4) * 128, 64)
+                share((c // 4) * 128 + 64, 64)
 
             @pl.when(c % 4 == 3)
             def _():
@@ -473,19 +474,19 @@
         return carry
 
     for h in range(2):
-        rows = pl.ds(128 * h, 128)
+        size = (192, 64)[h]
+        rows, tokens = pl.ds(192 * h, size), pl.ds(768 * h, 4 * size)
         local(ux.at[0, rows], ux.at[0, rows], own_s.at[1 + h]).wait()
         remote(ux.at[others, rows], ux.at[others, rows], dp_s.at[3], dp_r.at[4 + h], mp=m).wait_recv()
-        for k in range(4):
-            uxt[h, :, pl.ds(128 * k, 128)] = ux[k, rows, :].T
+        uxt[:, tokens] = ux[:, rows, :].reshape(4 * size, 512).T
         remote(gx.at[others, rows], gx.at[others, rows], dp_s.at[2], dp_r.at[2 + h], mp=m).wait_recv()
 
         def grad_tile(j, carry):
             cols = pl.ds(pl.multiple_of(j * 256, 256), 256)
             cols_up = pl.ds(pl.multiple_of(UNITS + j * 256, 256), 256)
-            down_sum = dot_nn(uxt[h], hx[:, rows, cols].reshape(2 * ROWS, 256))
-            gate_sum = dot_nn(ngt[h], gx[:, rows, cols].reshape(2 * ROWS, 256))
-            up_sum = dot_nn(ngt[h], gx[:, rows, cols_up].reshape(2 * ROWS, 256))
+            down_sum = dot_nn(uxt[:, tokens], hx[:, rows, cols].reshape(4 * size, 256))
+            gate_sum = dot_nn(ngt[:, tokens], gx[:, rows, cols].reshape(4 * size, 256))
+            up_sum = dot_nn(ngt[:, tokens], gx[:, rows, cols_up].reshape(4 * size, 256))
             if h == 0:
                 acc[0, :, cols] = down_sum
                 acc[1, :, cols] = gate_sum
@@ -591,8 +592,8 @@
             V((4, ROWS, UNITS), BF16),
             V((4, ROWS, 512), BF16),
             V((4, ROWS, 512), BF16),
-            V((2, 512, 2 * ROWS), BF16),
-            V((2, 512, 2 * ROWS), BF16),
+            V((512, 4 * ROWS), BF16),
+            V((512, 4 * ROWS), BF16),
             V((3, 512, UNITS), F32),
             V((CHUNKS, BLOCKS) + pieces, BF16),
             V((2, TURNS, 16) + pieces, BF16),

time: 86.7 us -> 86.1 us (level)
  no operation moved by 1% of the time
where the time goes in v5:
time: 86.1 us; the launch traced here: 85.9 us
  Pallas kernels  85.3 us (99%)
    pallas_call x1, Pallas kernels, on_device(): pl.pallas_call(kernel, out_shape=shapes, in_specs=[pl.BlockSpec(memory_sp...  83.6 us

profile of v5, /device:TPU:2, one launch (start us, length us, event | category | flops | bytes accessed | tf_op | source)
XLA Modules:
  0.0 85.9 jit_solution(6192838914245364110)
XLA Ops:
  0.6 83.6 %relay.1 = (bf16[1,256,2048]{2,1,0:T(8,128)(2,1)S(1)}, bf16[1,512,512]{2,1,0:T(8,128)(2,1)S(1)}, bf16[1,512,512]{2,1,0:T(8,128)(2,1)S(1)}, f32[1,512,512]{2,1,0:T(8,128)S(1)}) custom-call(bf16[1,256,2048]{2,1,0:T(8,128)(2,1)} %li_h.1, bf16[256,2048]{1,0:T(8,128)(2,1)} %tg_h.1, f32[1,2048]{1,0:T(1,128)} %gain_h.1, bf16[1,2048,512]{2,1,0:T(8,128)(2,1)} %gw_h.1, ...), custom_call_target="tpu_custom_call" | custom-call | tf_op jit(solution)/shard_map/relay/pallas_call | solution.py:572
  84.2 1.7 %hand_on.1 = (bf16[1,256,2048]{2,1,0:T(8,128)(2,1)}, bf16[1,512,512]{2,1,0:T(8,128)(2,1)}, bf16[1,512,512]{2,1,0:T(8,128)(2,1)}, f32[1,512,512]{2,1,0:T(8,128)}) custom-call(bf16[1,256,2048]{2,1,0:T(8,128)(2,1)S(1)} %get-tuple-element.8.refs_0_, bf16[1,512,512]{2,1,0:T(8,128)(2,1)S(1)} %get-tuple-element.9.refs_1_, ...), custom_call_target="tpu_custom_call" | custom-call | tf_op jit(solution)/shard_map/hand_on/pallas_call | solution.py:637

commit v6 on v5

--- a/solution.py
+++ b/solution.py
@@ -289,8 +289,8 @@
         own_ng.wait()
         remote(ngx.at[others], ngx.at[others], dp_s.at[0], dp_r.at[0], mp=m).wait_recv()
         for h in range(2):
-            size = (192, 64)[h]
-            ngt[:, pl.ds(768 * h, 4 * size)] = ngx[:, pl.ds(192 * h, size), :].reshape(4 * size, 512).T
+            size = (224, 32)[h]
+            ngt[:, pl.ds(896 * h, 4 * size)] = ngx[:, pl.ds(224 * h, size), :].reshape(4 * size, 512).T
 
     @pl.when(s < 3)
     def _():
@@ -380,7 +380,7 @@
 
     def share(start, size):
         rows = pl.ds(pl.multiple_of(start, CH), size)
-        half = start // 192
+        half = start // 224
         local(up.at[rows, feature_cols(0)], ux.at[0, rows], own_s.at[1 + half]).start()
         for k in (2, 1, 3):
             peer = lax.rem(d + k, 4)
@@ -399,8 +399,8 @@
 
         lax.fori_loop(0, CHUNKS, chunk_step, 0)
         bulk()
-        share(0, 192)
-        share(192, 64)
+        share(0, 224)
+        share(224, 32)
 
     @pl.when(s < 3)
     def _():
@@ -420,7 +420,8 @@
             @pl.when((s > 0) & (c % 4 == 3))
             def _():
                 share((c // 4) * 128, 64)
-                share((c // 4) * 128 + 64, 64)
+                share((c // 4) * 128 + 64, 32)
+                share((c // 4) * 128 + 96, 32)
 
             @pl.when(c % 4 == 3)
             def _():
@@ -474,8 +475,8 @@
         return carry
 
     for h in range(2):
-        size = (192, 64)[h]
-        rows, tokens = pl.ds(192 * h, size), pl.ds(768 * h, 4 * size)
+        size = (224, 32)[h]
+        rows, tokens = pl.ds(224 * h, size), pl.ds(896 * h, 4 * size)
         local(ux.at[0, rows], ux.at[0, rows], own_s.at[1 + h]).wait()
         remote(ux.at[others, rows], ux.at[others, rows], dp_s.at[3], dp_r.at[4 + h], mp=m).wait_recv()
         uxt[:, tokens] = ux[:, rows, :].reshape(4 * size, 512).T

time: 86.1 us -> 86.4 us (level)
  no operation moved by 1% of the time
where the time goes in v6:
time: 86.4 us; the launch traced here: 86.2 us
  Pallas kernels  85.6 us (99%)
    pallas_call x1, Pallas kernels, on_device(): pl.pallas_call(kernel, out_shape=shapes, in_specs=[pl.BlockSpec(memory_sp...  83.9 us

profile of v6, /device:TPU:2, one launch (start us, length us, event | category | flops | bytes accessed | tf_op | source)
XLA Modules:
  0.0 86.2 jit_solution(13401626151083374686)
XLA Ops:
  0.6 83.9 %relay.1 = (bf16[1,256,2048]{2,1,0:T(8,128)(2,1)S(1)}, bf16[1,512,512]{2,1,0:T(8,128)(2,1)S(1)}, bf16[1,512,512]{2,1,0:T(8,128)(2,1)S(1)}, f32[1,512,512]{2,1,0:T(8,128)S(1)}) custom-call(bf16[1,256,2048]{2,1,0:T(8,128)(2,1)} %li_h.1, bf16[256,2048]{1,0:T(8,128)(2,1)} %tg_h.1, f32[1,2048]{1,0:T(1,128)} %gain_h.1, bf16[1,2048,512]{2,1,0:T(8,128)(2,1)} %gw_h.1, ...), custom_call_target="tpu_custom_call" | custom-call | tf_op jit(solution)/shard_map/relay/pallas_call | solution.py:573
  84.5 1.7 %hand_on.1 = (bf16[1,256,2048]{2,1,0:T(8,128)(2,1)}, bf16[1,512,512]{2,1,0:T(8,128)(2,1)}, bf16[1,512,512]{2,1,0:T(8,128)(2,1)}, f32[1,512,512]{2,1,0:T(8,128)}) custom-call(bf16[1,256,2048]{2,1,0:T(8,128)(2,1)S(1)} %get-tuple-element.8.refs_0_, bf16[1,512,512]{2,1,0:T(8,128)(2,1)S(1)} %get-tuple-element.9.refs_1_, ...), custom_call_target="tpu_custom_call" | custom-call | tf_op jit(solution)/shard_map/hand_on/pallas_call | solution.py:638
